TPU v7x, 128 devices: a whole 4x4x4 slice. The times are simulated.
128 devices in a mesh: pipe: 2 (over core), expert: 16 (over x, y), tensor: 4 (over z).
Axes of the slice: x: 4, y: 4, z: 4, core: 2. Of those that a mesh axis runs over, the one named last changes fastest.
Arguments:
- block_input: bfloat16 [2, 2048, 768], P(None, 'expert'), may hold values from -6 to 6
- cotangent: bfloat16 [2, 2048, 768], P(None, 'expert'), may hold values from -6 to 6
- routes: int32 [2, 2, 2048, 2], P('pipe', None, 'expert'), may hold values from 0 to 31, all different within a row; in each aligned block of 128 rows (0 to 127, 128 to 255, ..., all dimensions but the last counted through in order) at most 8 rows name the same one
- offset_bucket: int32 [128], replicated, may hold values from 0 to 31
- norm1_gain: float32 [2, 768], P('pipe'), may hold values from 0.5 to 1.5
- qkv_weight: bfloat16 [2, 3, 768, 768], P('pipe', None, None, 'tensor'), may hold values from -0.21875 to 0.21875
- out_weight: bfloat16 [2, 768, 768], P('pipe', 'tensor'), may hold values from -0.875 to 0.875
- bias_table: float32 [2, 12, 32], P('pipe', 'tensor'), may hold values from -4 to 4
- norm2_gain: float32 [2, 768], P('pipe'), may hold values from 0.5 to 1.5
- router_weight: float32 [2, 768, 32], P('pipe'), may hold values from -0.3125 to 0.3125
- up_weight: bfloat16 [2, 32, 768, 3072], P('pipe', 'expert', None, 'tensor'), may hold values from -0.21875 to 0.21875
- down_weight: bfloat16 [2, 32, 3072, 768], P('pipe', 'expert', 'tensor'), may hold values from -0.109375 to 0.109375
Outputs:
- section_ends: float32 [2, 2, 2048, 768], P('pipe', None, 'expert')
- grad_norm1: float32 [2, 768], P('pipe')
- grad_qkv: float32 [2, 3, 768, 768], P('pipe', None, None, 'tensor')
- grad_out: float32 [2, 768, 768], P('pipe', 'tensor')
- grad_bias: float32 [2, 12, 32], P('pipe', 'tensor')
- grad_norm2: float32 [2, 768], P('pipe')
- grad_router: float32 [2, 768, 32], P('pipe')
- grad_up: float32 [2, 32, 768, 3072], P('pipe', 'expert', None, 'tensor')
- grad_down: float32 [2, 32, 3072, 768], P('pipe', 'expert', 'tensor')
Inputs may be any that keep to these rules, and one draw needn't show every extreme that they name: For each layer, micro-batch and sequence of 128 tokens, no expert is named by more than 8 routes, a bound that some block reaches. A token's two experts differ.
All inputs are finite; a program needn't handle non-finite values.
Results may differ from a plain program's by a relative error of at most 0.035.
Values may be sent and summed in bfloat16 or wider, within the bound.
A program may use at most 128 MiB of HBM per device.

v0:
```python
import jax
import jax.numpy as jnp
from jax import lax
from jax.sharding import PartitionSpec as P

EPS = 1e-06
MASKED = -1e30


def from_partner(x, axis, bit):
    return lax.ppermute(x, axis, [(i, i ^ 1 << bit) for i in range(lax.axis_size(axis))])


def copy_for_each(x, axis):
    copies = jnp.broadcast_to(x, (lax.axis_size(axis), *x.shape))
    return lax.all_to_all(copies, axis, split_axis=0, concat_axis=0, tiled=True)


def of_everyone(x, axis):
    everything = copy_for_each(x, axis)
    return jnp.sum(everything.astype(jnp.float32), axis=0)


def in_blocks(x, dim, size):
    shape = x.shape
    blocks = x.reshape(*shape[:dim], size, shape[dim] // size, *shape[dim + 1 :])
    return jnp.moveaxis(blocks, dim, 0)


def summed_on_arrival(x, axis, dim):
    blocks = in_blocks(x, dim, lax.axis_size(axis))
    arrived = lax.all_to_all(blocks, axis, split_axis=0, concat_axis=0, tiled=True)
    return arrived.astype(jnp.float32).sum(axis=0)


def rms_norm(values, gain_vec):
    return values * lax.rsqrt(jnp.mean(values * values, -1, keepdims=True) + EPS) * gain_vec


def gelu_tanh(values):
    return jax.nn.gelu(values, approximate=True)


def slot_rows(route_now, expert_total, capacity):
    flat_ids = route_now.reshape(-1)
    one_hot = (flat_ids[:, None] == jnp.arange(expert_total, dtype=jnp.int32)[None, :]).astype(
        jnp.int32
    )
    before = jnp.cumsum(one_hot, 0) - one_hot
    return flat_ids * capacity + jnp.sum(before * one_hot, 1)


def route_table(route_now, expert_total):
    return (
        route_now[:, :, None] == jnp.arange(expert_total, dtype=jnp.int32)[None, None, :]
    ).astype(jnp.float32)


def gate_of(normed, router, route_hot):
    logits = jnp.dot(normed, router, precision=lax.Precision.HIGHEST)
    expert_probs = jax.nn.softmax(logits, -1)
    chosen = jnp.sum(expert_probs[:, None, :] * route_hot, -1)
    return chosen / jnp.sum(chosen, -1, keepdims=True)


def diag_sums(score_grid):
    head_count, grid_length = (score_grid.shape[0], score_grid.shape[1])
    flipped = score_grid[:, ::-1, ::-1].reshape(head_count, grid_length * grid_length)
    padded = jnp.pad(flipped, ((0, 0), (0, grid_length))).reshape(
        head_count, grid_length, grid_length + 1
    )
    return jnp.sum(padded, 1)[:, :grid_length]


def cross_section(values):
    return from_partner(values, "pipe", 0)


def body(
    block_input,
    cotangent,
    routes,
    offset_bucket,
    norm1_gain,
    qkv_weight,
    out_weight,
    bias_table,
    norm2_gain,
    router_weight,
    up_weight,
    down_weight,
):
    section_index = lax.axis_index("pipe")
    expert_count = lax.axis_size("expert")
    tensor_count = lax.axis_size("tensor")
    micro_count, seq_len, model_width = block_input.shape
    top_count = routes.shape[-1]
    gain_one = norm1_gain[0]
    w_qkv = qkv_weight[0]
    w_out = out_weight[0]
    bias_rows = bias_table[0]
    gain_two = norm2_gain[0]
    router = router_weight[0]
    w_up = up_weight[0]
    w_down = down_weight[0]
    route_mine = routes[0]
    local_heads, bucket_count = bias_rows.shape
    head_size = w_qkv.shape[2] // local_heads
    score_scale = head_size ** (-0.5)
    expert_total = router.shape[1]
    local_experts = w_up.shape[0]
    capacity = tensor_count * max(1, seq_len * top_count * 4 // (3 * expert_total * tensor_count))
    positions = jnp.arange(seq_len, dtype=jnp.int32)
    offsets = jnp.clip(positions[:, None] - positions[None, :], 0, seq_len - 1)
    causal = positions[:, None] >= positions[None, :]
    bucket_hot = (
        offset_bucket[:, None] == jnp.arange(bucket_count, dtype=jnp.int32)[None, :]
    ).astype(jnp.float32)
    rel_bias = jnp.dot(bias_rows, bucket_hot.T, precision=lax.Precision.HIGHEST)[:, offsets]

    def scores_of(query_heads, key_heads):
        raw_scores = (
            jnp.einsum("hqd,hkd->hqk", query_heads, key_heads, preferred_element_type=jnp.float32)
            * score_scale
            + rel_bias
        )
        return jnp.where(causal[None], raw_scores, MASKED)

    def layer_backward(grad_out, saved):
        (
            h_in,
            n_one,
            query_heads,
            key_heads,
            value_heads,
            log_total,
            mixed_heads,
            h_mid,
            n_two,
            slot_dest,
            route_hot,
            arrived,
            lifted,
            picked,
        ) = saved
        gate_values, gate_pull = jax.vjp(
            lambda normed, weights: gate_of(normed, weights, route_hot),
            n_two.astype(jnp.float32),
            router,
        )
        grad_gates = jnp.sum(picked * grad_out[:, None, :], -1)
        grad_picked = (
            (gate_values[:, :, None] * grad_out[:, None, :])
            .astype(jnp.bfloat16)
            .reshape(seq_len * top_count, model_width)
        )
        grad_buffer = (
            jnp.zeros((expert_total * capacity, model_width), jnp.bfloat16)
            .at[slot_dest]
            .set(grad_picked)
        )
        grad_buffer = grad_buffer.reshape(expert_count, local_experts, capacity, model_width)
        grad_arrived = lax.all_to_all(
            grad_buffer, "expert", split_axis=0, concat_axis=0, tiled=True
        )
        hidden = gelu_tanh(lifted).astype(jnp.bfloat16)
        grad_down = jnp.einsum(
            "secf,secd->efd", hidden, grad_arrived, preferred_element_type=jnp.float32
        )
        grad_hidden = jnp.einsum(
            "secd,efd->secf", grad_arrived, w_down, preferred_element_type=jnp.float32
        )
        grad_lifted = jax.vjp(gelu_tanh, lifted)[1](grad_hidden)[0].astype(jnp.bfloat16)
        grad_up = jnp.einsum(
            "secd,secf->edf", arrived, grad_lifted, preferred_element_type=jnp.float32
        )
        grad_rows_part = jnp.einsum(
            "secf,edf->secd", grad_lifted, w_up, preferred_element_type=jnp.float32
        )
        grad_part = summed_on_arrival(grad_rows_part.astype(jnp.bfloat16), "tensor", 2).astype(
            jnp.bfloat16
        )
        grad_back = lax.all_to_all(grad_part, "expert", split_axis=0, concat_axis=0, tiled=True)
        grad_back = lax.all_gather(grad_back, "tensor", axis=2, tiled=True).reshape(
            expert_total * capacity, model_width
        )
        grad_n_two = jnp.sum(
            grad_back[slot_dest].astype(jnp.float32).reshape(seq_len, top_count, model_width), 1
        )
        grad_normed, grad_router = gate_pull(grad_gates)
        grad_n_two = grad_n_two + grad_normed
        grad_from_two, grad_gain_two = jax.vjp(rms_norm, h_mid, gain_two)[1](grad_n_two)
        grad_mid = grad_out + grad_from_two
        grad_attn = grad_mid.astype(jnp.bfloat16)
        grad_w_out = jnp.einsum(
            "tf,td->fd", mixed_heads, grad_attn, preferred_element_type=jnp.float32
        )
        grad_mixed = jnp.einsum(
            "td,fd->tf", grad_attn, w_out, preferred_element_type=jnp.float32
        ).astype(jnp.bfloat16)
        grad_mixed = grad_mixed.reshape(seq_len, local_heads, head_size).transpose(1, 0, 2)
        scores = scores_of(query_heads, key_heads)
        attn_probs = jnp.exp(scores - log_total)
        grad_value = jnp.einsum(
            "hqk,hqd->hkd",
            attn_probs.astype(jnp.bfloat16),
            grad_mixed,
            preferred_element_type=jnp.float32,
        ).astype(jnp.bfloat16)
        grad_probs = jnp.einsum(
            "hqd,hkd->hqk", grad_mixed, value_heads, preferred_element_type=jnp.float32
        )
        grad_scores = (
            attn_probs * (grad_probs - jnp.sum(attn_probs * grad_probs, -1, keepdims=True))
        ).astype(jnp.bfloat16)
        grad_query = (
            jnp.einsum("hqk,hkd->hqd", grad_scores, key_heads, preferred_element_type=jnp.float32)
            * score_scale
        ).astype(jnp.bfloat16)
        grad_key = (
            jnp.einsum("hqk,hqd->hkd", grad_scores, query_heads, preferred_element_type=jnp.float32)
            * score_scale
        ).astype(jnp.bfloat16)
        grad_table = jnp.dot(
            diag_sums(grad_scores.astype(jnp.float32)), bucket_hot, precision=lax.Precision.HIGHEST
        )
        grad_heads = (
            jnp.stack([grad_query, grad_key, grad_value])
            .transpose(0, 2, 1, 3)
            .reshape(3, seq_len, local_heads * head_size)
        )
        grad_w_qkv = jnp.einsum(
            "td,ctf->cdf", n_one, grad_heads, preferred_element_type=jnp.float32
        )
        grad_n_one = of_everyone(
            jnp.einsum("ctf,cdf->td", grad_heads, w_qkv, preferred_element_type=jnp.float32).astype(
                jnp.bfloat16
            ),
            "tensor",
        ).astype(jnp.float32)
        grad_from_one, grad_gain_one = jax.vjp(rms_norm, h_in, gain_one)[1](grad_n_one)
        weight_terms = (
            grad_gain_one,
            grad_w_qkv,
            grad_w_out,
            grad_table,
            grad_gain_two,
            grad_router,
            grad_up,
            grad_down,
        )
        return (grad_mid + grad_from_one, weight_terms)

    arriving = jnp.zeros((seq_len, model_width), jnp.float32)
    saved_list = []
    layer_outputs = []
    for step_index in range(micro_count + 1):
        own_input = block_input[min(step_index, micro_count - 1)].astype(jnp.float32)
        layer_input = jnp.where(section_index == 0, own_input, arriving)
        route_pick = jnp.clip(step_index - section_index, 0, micro_count - 1)
        route_now = lax.dynamic_index_in_dim(route_mine, route_pick, 0, keepdims=False)
        layer_slot_dest = slot_rows(route_now, expert_total, capacity)
        layer_route_hot = route_table(route_now, expert_total)
        layer_n_one = rms_norm(layer_input, gain_one).astype(jnp.bfloat16)
        qkv_rows = jnp.einsum(
            "td,cdf->ctf", layer_n_one, w_qkv, preferred_element_type=jnp.float32
        ).astype(jnp.bfloat16)
        qkv_heads = qkv_rows.reshape(3, seq_len, local_heads, head_size).transpose(0, 2, 1, 3)
        layer_query_heads = qkv_heads[0]
        layer_key_heads = qkv_heads[1]
        layer_value_heads = qkv_heads[2]
        layer_scores = scores_of(layer_query_heads, layer_key_heads)
        row_top = jnp.max(layer_scores, -1, keepdims=True)
        exp_scores = jnp.exp(layer_scores - row_top)
        row_total = jnp.sum(exp_scores, -1, keepdims=True)
        layer_log_total = row_top + jnp.log(row_total)
        layer_attn_probs = (exp_scores / row_total).astype(jnp.bfloat16)
        layer_mixed_heads = jnp.einsum(
            "hqk,hkd->hqd", layer_attn_probs, layer_value_heads, preferred_element_type=jnp.float32
        ).astype(jnp.bfloat16)
        layer_mixed_heads = layer_mixed_heads.transpose(1, 0, 2).reshape(
            seq_len, local_heads * head_size
        )
        attn_out = of_everyone(
            jnp.dot(layer_mixed_heads, w_out, preferred_element_type=jnp.float32).astype(
                jnp.bfloat16
            ),
            "tensor",
        ).astype(jnp.float32)
        layer_h_mid = layer_input + attn_out
        layer_n_two = rms_norm(layer_h_mid, gain_two).astype(jnp.bfloat16)
        layer_gate_values = gate_of(layer_n_two.astype(jnp.float32), router, layer_route_hot)
        buffer = (
            jnp.zeros((expert_total * capacity, model_width), jnp.bfloat16)
            .at[layer_slot_dest]
            .set(jnp.repeat(layer_n_two, top_count, 0))
        )
        buffer = buffer.reshape(expert_count, local_experts, capacity, model_width)
        layer_arrived = lax.all_to_all(buffer, "expert", split_axis=0, concat_axis=0, tiled=True)
        layer_lifted = jnp.einsum(
            "secd,edf->secf", layer_arrived, w_up, preferred_element_type=jnp.float32
        )
        layer_hidden = gelu_tanh(layer_lifted).astype(jnp.bfloat16)
        expert_part = jnp.einsum(
            "secf,efd->secd", layer_hidden, w_down, preferred_element_type=jnp.float32
        )
        summed_part = summed_on_arrival(expert_part.astype(jnp.bfloat16), "tensor", 2).astype(
            jnp.bfloat16
        )
        came_back = lax.all_to_all(summed_part, "expert", split_axis=0, concat_axis=0, tiled=True)
        came_back = lax.all_gather(came_back, "tensor", axis=2, tiled=True).reshape(
            expert_total * capacity, model_width
        )
        layer_picked = (
            came_back[layer_slot_dest].astype(jnp.float32).reshape(seq_len, top_count, model_width)
        )
        layer_out = layer_h_mid + jnp.sum(layer_gate_values[:, :, None] * layer_picked, 1)
        layer_saved = (
            layer_input,
            layer_n_one,
            layer_query_heads,
            layer_key_heads,
            layer_value_heads,
            layer_log_total,
            layer_mixed_heads,
            layer_h_mid,
            layer_n_two,
            layer_slot_dest,
            layer_route_hot,
            layer_arrived,
            layer_lifted,
            layer_picked,
        )
        layer_out, saved = (layer_out, layer_saved)
        saved_list.append(saved)
        layer_outputs.append(layer_out)
        if step_index < micro_count:
            arriving = cross_section(layer_out.astype(jnp.bfloat16)).astype(jnp.float32)
    arriving_grad = jnp.zeros((seq_len, model_width), jnp.float32)
    grad_inputs = []
    totals = None
    for step_index in range(micro_count + 1):
        earlier = saved_list[max(step_index - 1, 0)]
        later_saved = saved_list[min(step_index + 1, micro_count)]
        saved = jax.tree.map(
            lambda first_pick, second_pick: jnp.where(section_index == 0, first_pick, second_pick),
            earlier,
            later_saved,
        )
        own_grad = cotangent[min(step_index, micro_count - 1)].astype(jnp.float32)
        grad_out = jnp.where(section_index == 1, own_grad, arriving_grad)
        grad_in, weight_terms = layer_backward(grad_out, saved)
        live_step = jnp.where(section_index == 0, step_index >= 1, step_index < micro_count).astype(
            jnp.float32
        )
        if totals is None:
            totals = jax.tree.map(lambda term_now: live_step * term_now, weight_terms)
        else:
            totals = jax.tree.map(
                lambda running, term_now: running + live_step * term_now, totals, weight_terms
            )
        grad_inputs.append(grad_in)
        if step_index < micro_count:
            arriving_grad = cross_section(grad_in.astype(jnp.bfloat16)).astype(jnp.float32)
    (
        grad_gain_one,
        grad_w_qkv,
        grad_w_out,
        grad_table,
        grad_gain_two,
        grad_router,
        grad_up,
        grad_down,
    ) = totals
    grad_gain_one, grad_w_qkv, grad_w_out, grad_table, grad_gain_two, grad_router = (
        lax.psum(grad_gain_one.astype(jnp.bfloat16), "expert").astype(jnp.float32),
        lax.psum(grad_w_qkv.astype(jnp.bfloat16), "expert").astype(jnp.float32),
        lax.psum(grad_w_out.astype(jnp.bfloat16), "expert").astype(jnp.float32),
        lax.psum(grad_table.astype(jnp.bfloat16), "expert").astype(jnp.float32),
        lax.psum(grad_gain_two.astype(jnp.bfloat16), "expert").astype(jnp.float32),
        lax.psum(grad_router.astype(jnp.bfloat16), "expert").astype(jnp.float32),
    )
    section_ends = jnp.where(
        section_index == 0, jnp.stack(grad_inputs[1:]), jnp.stack(layer_outputs[1:])
    )[None]
    return (
        section_ends,
        grad_gain_one[None],
        grad_w_qkv[None],
        grad_w_out[None],
        grad_table[None],
        grad_gain_two[None],
        grad_router[None],
        grad_up[None],
        grad_down[None],
    )


def solution(mesh):
    in_specs = (
        P(None, "expert", None),
        P(None, "expert", None),
        P("pipe", None, "expert", None),
        P(),
        P("pipe", None),
        P("pipe", None, None, "tensor"),
        P("pipe", "tensor", None),
        P("pipe", "tensor", None),
        P("pipe", None),
        P("pipe", None, None),
        P("pipe", "expert", None, "tensor"),
        P("pipe", "expert", "tensor", None),
    )
    out_specs = (
        P("pipe", None, "expert", None),
        P("pipe", None),
        P("pipe", None, None, "tensor"),
        P("pipe", "tensor", None),
        P("pipe", "tensor", None),
        P("pipe", None),
        P("pipe", None, None),
        P("pipe", "expert", None, "tensor"),
        P("pipe", "expert", "tensor", None),
    )
    return jax.shard_map(body, mesh=mesh, in_specs=in_specs, out_specs=out_specs, check_vma=False)
```

profile of v0, /device:TPU:0, one launch (start us, length us, event | category | flops | bytes accessed | tf_op | source)
XLA Modules:
  0.0 800.7 jit_solution(6305286920345469587)
XLA Ops:
  12.1 54.4 %gather_fusion = f32[16384,3]{1,0:T(8,128)} fusion(f32[3,128]{0,1:T(8,128)S(1)} %copy.365, s32[16384]{0:T(1024)S(1)} %fusion.324), kind=kCustom, calls=%fused_computation | custom fusion | bytes 458752 | tf_op jit(solution)/shard_map/gather | solution.py:119
  66.5 6.6 copy.367
  75.2 5.5 all-to-all-start
  101.8 7.1 all-to-all-start.1
  110.4 7.6 all-to-all-done.1
  128.0 5.9 all-to-all-done.2
  139.6 7.0 all-to-all-done.3
  146.6 12.7 %all_gather.18 = bf16[16,2,8,768]{3,0,1,2:T(8,128)(2,1)S(1)} all-gather(bf16[16,2,2,768]{3,0,1,2:T(8,128)(2,1)S(1)} %copy.374), channel_id=1, replica_groups=mesh['pipe'=2,'expert'=16,'tensor'=4] {'tensor'}, dimensions={2}, use_global_device_ids=true | all-gather | bytes 491520 | tf_op jit(solution)/shard_map/all_gather | solution.py:311
  208.7 6.0 all-to-all-done.6
  228.5 5.4 all-to-all-done.9
  248.2 12.8 %all_gather.20 = bf16[16,2,8,768]{3,0,1,2:T(8,128)(2,1)S(1)} all-gather(bf16[16,2,2,768]{3,0,1,2:T(8,128)(2,1)S(1)} %copy.388), channel_id=1, replica_groups=mesh['pipe'=2,'expert'=16,'tensor'=4] {'tensor'}, dimensions={2}, use_global_device_ids=true | all-gather | bytes 491520 | tf_op jit(solution)/shard_map/all_gather | solution.py:311
  288.2 6.4 all-to-all-done.5
  326.9 12.9 %all_gather.19 = bf16[16,2,8,768]{3,0,1,2:T(8,128)(2,1)S(1)} all-gather(bf16[16,2,2,768]{3,0,1,2:T(8,128)(2,1)S(1)} %copy.383), channel_id=1, replica_groups=mesh['pipe'=2,'expert'=16,'tensor'=4] {'tensor'}, dimensions={2}, use_global_device_ids=true | all-gather | bytes 491520 | tf_op jit(solution)/shard_map/all_gather | solution.py:184
  419.4 6.1 all-to-all-done.14
  439.4 5.4 all-to-all-done.17
  453.8 5.2 all-to-all-done.18
  459.1 12.7 %all_gather.22 = bf16[16,2,8,768]{3,0,1,2:T(8,128)(2,1)S(1)} all-gather(bf16[16,2,2,768]{3,0,1,2:T(8,128)(2,1)S(1)} %copy.412), channel_id=1, replica_groups=mesh['pipe'=2,'expert'=16,'tensor'=4] {'tensor'}, dimensions={2}, use_global_device_ids=true | all-gather | bytes 491520 | tf_op jit(solution)/shard_map/all_gather | solution.py:311
  487.3 7.6 all-to-all-done.13
  527.0 12.7 %all_gather.21 = bf16[16,2,8,768]{3,0,1,2:T(8,128)(2,1)S(1)} all-gather(bf16[16,2,2,768]{3,0,1,2:T(8,128)(2,1)S(1)} %copy.407), channel_id=1, replica_groups=mesh['pipe'=2,'expert'=16,'tensor'=4] {'tensor'}, dimensions={2}, use_global_device_ids=true | all-gather | bytes 491520 | tf_op jit(solution)/shard_map/all_gather | solution.py:184
  609.1 5.6 all-to-all-done.20
  626.6 7.3 fusion.1
  641.9 7.1 fusion.3
  650.6 13.6 %all_gather.23 = bf16[16,2,8,768]{3,0,1,2:T(8,128)(2,1)S(1)} all-gather(bf16[16,2,2,768]{3,0,1,2:T(8,128)(2,1)S(1)} %copy.424), channel_id=1, replica_groups=mesh['pipe'=2,'expert'=16,'tensor'=4] {'tensor'}, dimensions={2}, use_global_device_ids=true | all-gather | bytes 491520 | tf_op jit(solution)/shard_map/all_gather | solution.py:184
  705.0 75.4 %all-reduce.3 = (bf16[1,3,32]{2,1,0:T(4,128)(2,1)}, bf16[1,768]{1,0:T(2,128)(2,1)}, bf16[1,768]{1,0:T(2,128)(2,1)S(1)}, bf16[1,768,32]{1,2,0:T(8,128)(2,1)}) all-reduce(bf16[1,3,32]{2,1,0:T(4,128)(2,1)} %fusion.127, bf16[1,768]{1,0:T(2,128)(2,1)S(1)} %broadcast_in_dim.274, ...), channel_id=1, replica_groups=mesh['pipe'=2,'expert'=16,'tensor'=4] {'expert'}, use_global_device_ids=true, to_apply=%region_105.106 | all-reduce | flops 26208 | bytes 104832 | tf_op jit(solution)/shard_map/psum | solution.py:379
  (702 shorter events, 474.5 us)
Async XLA Ops:
  75.2 17.9 %all-to-all-start = ((bf16[4,128,768]{2,1,0:T(8,128)(2,1)}), bf16[4,128,768]{2,1,0:T(8,128)(2,1)}, u32[]{:S(2)}, u32[]{:S(2)}) async-start(bf16[4,128,768]{2,1,0:T(8,128)(2,1)} %broadcast_in_dim.126), calls=%async_computation | async-start | bytes 1572864 | tf_op jit(solution)/shard_map/all_to_all | solution.py:16
  101.8 16.3 %all-to-all-start.1 = ((bf16[16,2,8,768]{3,2,1,0:T(8,128)(2,1)}), bf16[16,2,8,768]{3,2,1,0:T(8,128)(2,1)}, u32[]{:S(2)}, u32[]{:S(2)}) async-start(bf16[16,2,8,768]{3,2,1,0:T(8,128)(2,1)} %bitcast.793), calls=%async_computation.1 | async-start | bytes 786432 | tf_op jit(solution)/shard_map/all_to_all | solution.py:299
  123.1 10.8 %all-to-all-start.2 = ((bf16[4,16,2,2,768]{4,3,1,2,0:T(2,128)(2,1)}), bf16[4,16,2,2,768]{4,3,1,2,0:T(2,128)(2,1)S(1)}, u32[]{:S(2)}, u32[]{:S(2)}) async-start(bf16[4,16,2,2,768]{4,3,1,2,0:T(2,128)(2,1)} %bitcast.740), calls=%async_computation.2 | async-start | bytes 786432 | tf_op jit(solution)/shard_map/all_to_all | solution.py:32
  135.1 11.5 %all-to-all-start.3 = ((bf16[16,2,2,768]{3,2,1,0:T(2,128)(2,1)}), bf16[16,2,2,768]{3,2,1,0:T(2,128)(2,1)S(1)}, u32[]{:S(2)}, u32[]{:S(2)}) async-start(bf16[16,2,2,768]{3,2,1,0:T(2,128)(2,1)} %copy.373), calls=%async_computation.3 | async-start | bytes 196608 | tf_op jit(solution)/shard_map/all_to_all | solution.py:310
  171.1 17.1 %all-to-all-start.4 = ((bf16[4,128,768]{2,1,0:T(8,128)(2,1)}), bf16[4,128,768]{2,1,0:T(8,128)(2,1)}, u32[]{:S(2)}, u32[]{:S(2)}) async-start(bf16[4,128,768]{2,1,0:T(8,128)(2,1)} %broadcast_in_dim.128), calls=%async_computation.4 | async-start | bytes 1572864 | tf_op jit(solution)/shard_map/all_to_all | solution.py:16
  201.7 13.0 %all-to-all-start.6 = ((bf16[16,2,8,768]{3,2,1,0:T(8,128)(2,1)}), bf16[16,2,8,768]{3,2,1,0:T(8,128)(2,1)S(1)}, u32[]{:S(2)}, u32[]{:S(2)}) async-start(bf16[16,2,8,768]{3,2,1,0:T(8,128)(2,1)} %bitcast.794), calls=%async_computation.6 | async-start | bytes 786432 | tf_op jit(solution)/shard_map/all_to_all | solution.py:299
  223.1 10.8 %all-to-all-start.9 = ((bf16[4,16,2,2,768]{4,3,1,2,0:T(2,128)(2,1)}), bf16[4,16,2,2,768]{4,3,1,2,0:T(2,128)(2,1)S(1)}, u32[]{:S(2)}, u32[]{:S(2)}) async-start(bf16[4,16,2,2,768]{4,3,1,2,0:T(2,128)(2,1)} %bitcast.795), calls=%async_computation.9 | async-start | bytes 786432 | tf_op jit(solution)/shard_map/all_to_all | solution.py:32
  236.6 11.5 %all-to-all-start.10 = ((bf16[16,2,2,768]{3,2,1,0:T(2,128)(2,1)}), bf16[16,2,2,768]{3,2,1,0:T(2,128)(2,1)S(1)}, u32[]{:S(2)}, u32[]{:S(2)}) async-start(bf16[16,2,2,768]{3,2,1,0:T(2,128)(2,1)} %copy.387), calls=%async_computation.10 | async-start | bytes 196608 | tf_op jit(solution)/shard_map/all_to_all | solution.py:310
  281.3 13.3 %all-to-all-start.5 = ((bf16[16,2,8,768]{3,2,1,0:T(8,128)(2,1)}), bf16[16,2,8,768]{3,2,1,0:T(8,128)(2,1)}, u32[]{:S(2)}, u32[]{:S(2)}) async-start(bf16[16,2,8,768]{3,2,1,0:T(8,128)(2,1)} %bitcast.59), calls=%async_computation.5 | async-start | bytes 786432 | tf_op jit(solution)/shard_map/all_to_all | solution.py:163
  286.4 88.6 %collective-permute-start.2 = (bf16[128,768]{1,0:T(8,128)(2,1)}, bf16[128,768]{1,0:T(8,128)(2,1)S(1)}, u32[]{:S(2)}, u32[]{:S(2)}) collective-permute-start(bf16[128,768]{1,0:T(8,128)(2,1)} %get-tuple-element.127), channel_id=1, source_target_pairs={{0,64},{64,0},{1,65},{65,1},{2,66},{66,2},{3,67},{67,3},{4,68},{68... | collective-permute-start | bytes 589832 | tf_op jit(solution)/shard_map/ppermute | solution.py:11
  301.7 11.6 %all-to-all-start.7 = ((bf16[4,16,2,2,768]{4,3,1,2,0:T(2,128)(2,1)}), bf16[4,16,2,2,768]{4,3,1,2,0:T(2,128)(2,1)}, u32[]{:S(2)}, u32[]{:S(2)}) async-start(bf16[4,16,2,2,768]{4,3,1,2,0:T(2,128)(2,1)} %bitcast.739), calls=%async_computation.7 | async-start | bytes 786432 | tf_op jit(solution)/shard_map/all_to_all | solution.py:32
  315.4 11.5 %all-to-all-start.8 = ((bf16[16,2,2,768]{3,2,1,0:T(2,128)(2,1)}), bf16[16,2,2,768]{3,2,1,0:T(2,128)(2,1)S(1)}, u32[]{:S(2)}, u32[]{:S(2)}) async-start(bf16[16,2,2,768]{3,2,1,0:T(2,128)(2,1)} %copy.382), calls=%async_computation.8 | async-start | bytes 196608 | tf_op jit(solution)/shard_map/all_to_all | solution.py:183
  355.0 18.5 %all-to-all-start.11 = ((bf16[4,128,768]{2,1,0:T(8,128)(2,1)}), bf16[4,128,768]{2,1,0:T(8,128)(2,1)}, u32[]{:S(2)}, u32[]{:S(2)}) async-start(bf16[4,128,768]{2,1,0:T(8,128)(2,1)} %broadcast_in_dim.258), calls=%async_computation.11 | async-start | bytes 1572864 | tf_op jit(solution)/shard_map/all_to_all | solution.py:16
  380.5 17.8 %all-to-all-start.12 = ((bf16[4,128,768]{2,1,0:T(8,128)(2,1)}), bf16[4,128,768]{2,1,0:T(8,128)(2,1)}, u32[]{:S(2)}, u32[]{:S(2)}) async-start(bf16[4,128,768]{2,1,0:T(8,128)(2,1)} %broadcast_in_dim.260), calls=%async_computation.12 | async-start | bytes 1572864 | tf_op jit(solution)/shard_map/all_to_all | solution.py:16
  412.2 13.3 %all-to-all-start.14 = ((bf16[16,2,8,768]{3,2,1,0:T(8,128)(2,1)}), bf16[16,2,8,768]{3,2,1,0:T(8,128)(2,1)S(1)}, u32[]{:S(2)}, u32[]{:S(2)}) async-start(bf16[16,2,8,768]{3,2,1,0:T(8,128)(2,1)} %bitcast.797), calls=%async_computation.14 | async-start | bytes 786432 | tf_op jit(solution)/shard_map/all_to_all | solution.py:299
  447.5 11.5 %all-to-all-start.18 = ((bf16[16,2,2,768]{3,2,1,0:T(2,128)(2,1)}), bf16[16,2,2,768]{3,2,1,0:T(2,128)(2,1)S(1)}, u32[]{:S(2)}, u32[]{:S(2)}) async-start(bf16[16,2,2,768]{3,2,1,0:T(2,128)(2,1)} %copy.411), calls=%async_computation.18 | async-start | bytes 196608 | tf_op jit(solution)/shard_map/all_to_all | solution.py:310
  481.6 13.4 %all-to-all-start.13 = ((bf16[16,2,8,768]{3,2,1,0:T(8,128)(2,1)}), bf16[16,2,8,768]{3,2,1,0:T(8,128)(2,1)}, u32[]{:S(2)}, u32[]{:S(2)}) async-start(bf16[16,2,8,768]{3,2,1,0:T(8,128)(2,1)} %bitcast.99), calls=%async_computation.13 | async-start | bytes 786432 | tf_op jit(solution)/shard_map/all_to_all | solution.py:163
  515.5 11.5 %all-to-all-start.16 = ((bf16[16,2,2,768]{3,2,1,0:T(2,128)(2,1)}), bf16[16,2,2,768]{3,2,1,0:T(2,128)(2,1)S(1)}, u32[]{:S(2)}, u32[]{:S(2)}) async-start(bf16[16,2,2,768]{3,2,1,0:T(2,128)(2,1)} %copy.406), calls=%async_computation.16 | async-start | bytes 196608 | tf_op jit(solution)/shard_map/all_to_all | solution.py:183
  554.9 19.2 %all-to-all-start.19 = ((bf16[4,128,768]{2,1,0:T(8,128)(2,1)}), bf16[4,128,768]{2,1,0:T(8,128)(2,1)}, u32[]{:S(2)}, u32[]{:S(2)}) async-start(bf16[4,128,768]{2,1,0:T(8,128)(2,1)} %broadcast_in_dim.266), calls=%async_computation.19 | async-start | bytes 1572864 | tf_op jit(solution)/shard_map/all_to_all | solution.py:16
  599.9 14.8 %all-to-all-start.20 = ((bf16[16,2,8,768]{3,2,1,0:T(8,128)(2,1)}), bf16[16,2,8,768]{3,2,1,0:T(8,128)(2,1)}, u32[]{:S(2)}, u32[]{:S(2)}) async-start(bf16[16,2,8,768]{3,2,1,0:T(8,128)(2,1)} %bitcast.791), calls=%async_computation.20 | async-start | bytes 786432 | tf_op jit(solution)/shard_map/all_to_all | solution.py:163
  621.8 12.2 %all-to-all-start.21 = ((bf16[4,16,2,2,768]{4,3,1,2,0:T(2,128)(2,1)}), bf16[4,16,2,2,768]{4,3,1,2,0:T(2,128)(2,1)}, u32[]{:S(2)}, u32[]{:S(2)}) async-start(bf16[4,16,2,2,768]{4,3,1,2,0:T(2,128)(2,1)} %bitcast.735), calls=%async_computation.21 | async-start | bytes 786432 | tf_op jit(solution)/shard_map/all_to_all | solution.py:32
  637.8 11.9 %all-to-all-start.22 = ((bf16[16,2,2,768]{3,2,1,0:T(2,128)(2,1)}), bf16[16,2,2,768]{3,2,1,0:T(2,128)(2,1)}, u32[]{:S(2)}, u32[]{:S(2)}) async-start(bf16[16,2,2,768]{3,2,1,0:T(2,128)(2,1)} %copy.423), calls=%async_computation.22 | async-start | bytes 196608 | tf_op jit(solution)/shard_map/all_to_all | solution.py:183
  687.2 13.7 %all-to-all-start.23 = ((bf16[4,128,768]{2,1,0:T(8,128)(2,1)}), bf16[4,128,768]{2,1,0:T(8,128)(2,1)}, u32[]{:S(2)}, u32[]{:S(2)}) async-start(bf16[4,128,768]{2,1,0:T(8,128)(2,1)} %broadcast_in_dim.272), calls=%async_computation.23 | async-start | bytes 1572864 | tf_op jit(solution)/shard_map/all_to_all | solution.py:16
  691.4 97.7 %all-reduce.7.cloned.1.call-start = ((), (), s32[]{:S(2)}) async-start(), calls=%async_computation.24 | async-start | bytes 2359296 | tf_op jit(solution)/shard_map/psum | solution.py:377
  (162 other events, 1296.0 us)
Sparse Core Ops, SparseCore 0:
  696.9 88.2 all-reduce.6
where the time goes:
time: 814 us; the launch traced here: 801 us
  local copies, waits for them, and re-layouts  186 us (23%)
  blocking collectives  153 us (19%)
  other arithmetic  134 us (16%)
  waiting for transfers between devices  107 us (13%)
  matrix products  105 us (13%)
  starting transfers between devices  100 us (12%)
  between operations  16.8 us (2%)
    psum x1, blocking collectives, body(): lax.psum(grad_table.astype(jnp.bfloat16), 'expert').astype(jnp.float32)  75.4 us
    gather x2, local copies, waits for them, and re-layouts, body(): jnp.dot(bias_rows, bucket_hot.T, precision=lax.Precision.HIGHEST)  61 us
    all_gather x3, blocking collectives, layer_backward(): lax.all_gather(grad_back, 'tensor', axis=2, tiled=True)  39.3 us
    all_gather x3, blocking collectives, body(): lax.all_gather(came_back, 'tensor', axis=2, tiled=True)  38.2 us
    all_to_all x6, starting transfers between devices, copy_for_each(): return lax.all_to_all(copies, axis, split_axis=0, concat_axis=0, tiled=True)  27 us
    all_to_all x6, waiting for transfers between devices, summed_on_arrival(): lax.all_to_all(blocks, axis, split_axis=0, concat_axis=0, tiled=True)  24.6 us
    all_to_all x6, starting transfers between devices, summed_on_arrival(): lax.all_to_all(blocks, axis, split_axis=0, concat_axis=0, tiled=True)  22.7 us
    all_to_all x3, waiting for transfers between devices, body(): lax.all_to_all(buffer, 'expert', split_axis=0, concat_axis=0, tiled=True)  19.8 us
  transfers between devices with their start and end apart: 29, of which 24 were waited for; matrix products, arithmetic and copies ran while one was open for 20% of the time, Pallas kernels for 0%

commit v1 on v0

v1 whole, which is shorter than its diff:
```python
import functools

import jax
import jax.numpy as jnp
from jax import lax
from jax.experimental import pallas as pl
from jax.experimental.pallas import tpu as pltpu
from jax.sharding import PartitionSpec as P

EPS = 1e-06
MASKED = -1e30
MESH = pl.DeviceIdType.MESH
F32 = jnp.float32
BF16 = jnp.bfloat16
LANES = 128
CAP = 8
TANH_A = 0.7978845608
TANH_B = 0.044715


def dot(a, b, left, right):
    return lax.dot_general(a, b, (((left,), (right,)), ((), ())), preferred_element_type=F32)


def nn(a, b):
    return dot(a, b, 1, 0)


def nt(a, b):
    return dot(a, b, 1, 1)


def tn(a, b):
    return dot(a, b, 0, 0)


def lanes_of(shape, dim):
    return lax.broadcasted_iota(jnp.int32, shape, dim)


def kernel(
    dims,
    x_in, cot_in, routes_in, hot_in, gain_in, rel_in, router_in, qkv_in, out_in, up_in, down_in,
    sec_out, own_out, recv_out, attn_out, small_out,
    xin, cot, hot, routes, gain, rel, router, w_qkv, w_out, w_up, w_down,
    hs, n_one, qkv, probs_s, mixed_s, h_mid_s, n_two, comb, eprobs, x_s, u_s, y_s, x_dy, x_du, x_hid, g_s, fin, dqkv,
    send_a, recv_a, red_a, red_g, grads, chunk, chunk_in, small, small_in, shard, shard_small, pair, pair_small,
    total, total_small,
    sem_in, sem_w, sem_ws, sa_send, sa_recv, rd_send, rd_recv, gr_send, gr_recv, gr_loc,
    ck_send, ck_recv, sm_send, sm_recv, pr_send, pr_recv, ag_send, ag_recv, ag_loc, sec_send, sec_recv, sec_loc,
):
    ne, nz, seq, width, local, heads, ff, hd = dims
    p = lax.axis_index("pipe")
    x = lax.axis_index("expert")
    z = lax.axis_index("tensor")
    other = 1 - p
    slots = ne * 2 * CAP
    hw = heads * hd
    rows = width // ne

    barrier = pltpu.get_barrier_semaphore()

    def hello_e(r, _):
        pl.semaphore_signal(barrier, inc=1, device_id={"expert": lax.rem(x + r, ne)}, device_id_type=MESH)
        return 0

    def hello_z(r, _):
        pl.semaphore_signal(barrier, inc=1, device_id={"tensor": lax.rem(z + r, nz)}, device_id_type=MESH)
        return 0

    lax.fori_loop(1, ne, hello_e, 0)
    lax.fori_loop(1, nz, hello_z, 0)
    pl.semaphore_signal(barrier, inc=1, device_id={"pipe": other}, device_id_type=MESH)

    ins = [
        pltpu.make_async_copy(x_in.at[p], xin, sem_in.at[0]),
        pltpu.make_async_copy(cot_in.at[p], cot, sem_in.at[1]),
        pltpu.make_async_copy(hot_in, hot, sem_in.at[2]),
    ]
    for copy in ins:
        copy.start()
    weights = [
        (gain_in, gain), (qkv_in, w_qkv), (rel_in, rel), (out_in, w_out), (router_in, router), (routes_in, routes),
        (up_in, w_up), (down_in, w_down),
    ]
    for k, (src, dst) in enumerate(weights):
        pltpu.make_async_copy(src.at[p] if k == 5 else src, dst.at[p], sem_w.at[k, p]).start()
    pl.semaphore_wait(barrier, ne - 1 + nz - 1 + 1)
    outgoing = []
    for k, (src, dst) in enumerate(weights):
        copy = pltpu.make_async_remote_copy(
            src_ref=src.at[other] if k == 5 else src, dst_ref=dst.at[p], send_sem=sem_ws.at[k], recv_sem=sem_w.at[k, p],
            device_id={"pipe": other}, device_id_type=MESH)
        copy.start()
        outgoing.append(copy)

    def await_weight(k, l):
        dst = weights[k][1]
        pltpu.make_async_copy(dst.at[l], dst.at[l], sem_w.at[k, l]).wait()

    def exchange(kind, l):
        def one(r, _):
            pltpu.make_async_remote_copy(
                src_ref=send_a.at[l, kind, r], dst_ref=recv_a.at[l, kind, r],
                send_sem=sa_send.at[l, kind], recv_sem=sa_recv.at[l, kind],
                device_id={"expert": lax.rem(x + r if kind % 2 == 0 else x + ne - r, ne)}, device_id_type=MESH).start()
            return 0
        lax.fori_loop(1, ne, one, 0)
        recv_a[l, kind, 0] = send_a[l, kind, 0]

    def arrived(kind, l):
        part = send_a.at[l, kind, pl.ds(1, ne - 1)]
        pltpu.make_async_copy(part, part, sa_send.at[l, kind]).wait()
        part = recv_a.at[l, kind, pl.ds(1, ne - 1)]
        pltpu.make_async_copy(part, part, sa_recv.at[l, kind]).wait()
        return recv_a[l, kind]

    def reduce_start(buf, at, sem):
        def one(r, _):
            pltpu.make_async_remote_copy(
                src_ref=buf.at[(*at, 0)], dst_ref=buf.at[(*at, r)], send_sem=rd_send.at[sem], recv_sem=rd_recv.at[sem],
                device_id={"tensor": lax.rem(z + r, nz)}, device_id_type=MESH).start()
            return 0
        lax.fori_loop(1, nz, one, 0)

    def reduce_end(buf, at, sem):
        part = buf.at[(*at, pl.ds(1, nz - 1))]
        pltpu.make_async_copy(part, part, rd_send.at[sem]).wait()
        pltpu.make_async_copy(part, part, rd_recv.at[sem]).wait()
        acc = None
        for a in range(nz):
            term = buf[(*at, lax.rem(z + nz - a, nz))].astype(F32)
            acc = term if acc is None else acc + term
        return acc

    def split(blocks):
        wide = blocks.astype(F32)
        return [wide[:, e * CAP:(e + 1) * CAP].reshape(ne * CAP, width).astype(BF16) for e in range(local)]

    def join(parts):
        return jnp.concatenate([part.reshape(ne, CAP, width) for part in parts], axis=1).astype(BF16)

    def head_mask(h):
        at = lanes_of((1, hw), 1)
        return ((at >= h * hd) & (at < (h + 1) * hd)).astype(BF16)

    def scale_of(h):
        return lax.rsqrt(jnp.mean(h * h, -1, keepdims=True) + EPS)

    def chosen_of(l):
        ids = routes[l]
        at = lanes_of((seq, LANES), 1)
        return [(at == ids[:, k:k + 1]).astype(F32) for k in range(2)]

    def forward(l, _):
        h_in = hs[l]
        await_weight(0, l)
        n1 = (h_in * scale_of(h_in) * gain[l, 0:1]).astype(BF16)
        n_one[l] = n1
        await_weight(1, l)
        for c in range(3):
            qkv[l, c] = nn(n1, w_qkv[l, c]).astype(BF16)
        q, k, v = qkv[l, 0], qkv[l, 1], qkv[l, 2]
        await_weight(2, l)
        causal = lanes_of((seq, seq), 0) >= lanes_of((seq, seq), 1)
        mixed = jnp.zeros((seq, hw), F32)
        for h in range(heads):
            mask = head_mask(h)
            bias = pltpu.roll(jnp.broadcast_to(rel[l, h:h + 1], (seq, seq)), 0, 1, stride=1, stride_axis=0)
            s = nt(q * mask, k) * (hd ** -0.5) + bias
            s = jnp.where(causal, s, MASKED)
            e = jnp.exp(s - jnp.max(s, -1, keepdims=True))
            prob = e / jnp.sum(e, -1, keepdims=True)
            probs_s[l, h] = prob
            mixed = mixed + nn(prob.astype(BF16), v * mask)
        mixed = mixed.astype(BF16)
        mixed_s[l] = mixed
        await_weight(3, l)
        red_a[l, 0, 0] = nn(mixed, w_out[l]).astype(BF16)
        reduce_start(red_a, (l, 0), l)

        await_weight(5, l)
        ids = routes[l]
        hot_e = chosen_of(l)
        row_at, col_at = lanes_of((seq, seq), 0), lanes_of((seq, seq), 1)
        earlier = (row_at > col_at).astype(BF16)
        count = nn(earlier, (hot_e[0] + hot_e[1]).astype(BF16))
        for kk in range(2):
            before = count if kk == 0 else count + hot_e[0]
            c = jnp.sum(before * hot_e[kk], -1, keepdims=True).astype(jnp.int32)
            e = ids[:, kk:kk + 1]
            place = (((e >> 1) - x + ne) & (ne - 1)) * (2 * CAP) + (e & 1) * CAP + c
            comb[l, kk * seq:(kk + 1) * seq] = (lanes_of((seq, slots), 1) == place).astype(F32).astype(BF16)
        both = comb[l, 0:seq] + comb[l, seq:2 * seq]
        await_weight(4, l)

        h_mid = h_in + reduce_end(red_a, (l, 0), l)
        h_mid_s[l] = h_mid
        n2 = (h_mid * scale_of(h_mid) * gain[l, 1:2]).astype(BF16)
        n_two[l] = n2
        send_a[l, 0] = tn(both, n2).astype(BF16).reshape(ne, 2 * CAP, width)
        exchange(0, l)
        wide = nn(n2, router[l])
        logits = wide[:, :LANES] + wide[:, LANES:]
        logits = jnp.where(lanes_of((seq, LANES), 1) < ne * local, logits, MASKED)
        e = jnp.exp(logits - jnp.max(logits, -1, keepdims=True))
        ep = e / jnp.sum(e, -1, keepdims=True)
        eprobs[l] = ep
        picked = [jnp.sum(ep * hot_e[kk], -1, keepdims=True) for kk in range(2)]
        inv = picked[0] + picked[1]
        gates = [picked[kk] / inv for kk in range(2)]
        await_weight(6, l)
        await_weight(7, l)
        parts = split(arrived(0, l))
        for e in range(local):
            x_s[l, e] = parts[e]

        def expert(e, _):
            u = nn(x_s[l, e], w_up[l, e])
            u_s[l, e] = u
            t = jnp.tanh(TANH_A * (u + TANH_B * u * u * u))
            y_s[e] = nn((0.5 * u * (1.0 + t)).astype(BF16), w_down[l, e])
            return 0
        lax.fori_loop(0, local, expert, 0)
        send_a[l, 1] = join([y_s[e] for e in range(local)])
        exchange(1, l)
        back = arrived(1, l).reshape(slots, width)
        got = gates[0] * nn(comb[l, 0:seq], back) + gates[1] * nn(comb[l, seq:2 * seq], back)
        red_a[l, 1, 0] = got.astype(BF16)
        reduce_start(red_a, (l, 1), 2 + l)
        out = h_mid + reduce_end(red_a, (l, 1), 2 + l)
        hs[l + 1] = jnp.where(l == 0, out.astype(BF16).astype(F32), out)
        return 0

    for copy in ins:
        copy.wait()
    hs[0] = xin[...].astype(F32)
    lax.fori_loop(0, 2, forward, 0)

    def deliver(src, owner):
        @pl.when(p == owner)
        def _():
            pltpu.make_async_copy(src, sec_out.at[p], sec_loc).start()

        @pl.when(p != owner)
        def _():
            pltpu.make_async_remote_copy(
                src_ref=src, dst_ref=sec_out.at[p], send_sem=sec_send, recv_sem=sec_recv,
                device_id={"pipe": other}, device_id_type=MESH).start()

    deliver(hs.at[2], 1)
    g_s[...] = cot[...].astype(F32)

    def backward(i, _):
        l = 1 - i
        g = g_s[...]
        hot_e = chosen_of(l)
        ep = eprobs[l]
        picked = [jnp.sum(ep * hot_e[kk], -1, keepdims=True) for kk in range(2)]
        inv = picked[0] + picked[1]
        gates = [picked[kk] / inv for kk in range(2)]
        dy = jnp.concatenate([(gates[kk] * g).astype(BF16) for kk in range(2)], axis=0)
        send_a[l, 2] = tn(comb[l], dy).astype(BF16).reshape(ne, 2 * CAP, width)
        exchange(2, l)
        back = recv_a[l, 1].reshape(slots, width)
        at = lanes_of((seq, LANES), 1)
        gg = jnp.zeros((seq, LANES), F32)
        for kk in range(2):
            part = jnp.sum(g * nn(comb[l, kk * seq:(kk + 1) * seq], back), -1, keepdims=True)
            high = part.astype(BF16).astype(F32)
            gg = gg + jnp.where(at == kk, high, 0.0) + jnp.where(at == 2 + kk, part - high, 0.0)
        red_g[l, 0, :, width:] = gg.astype(BF16)
        parts = split(arrived(2, l))
        for e in range(local):
            x_dy[e] = parts[e]

        def expert(e, _):
            dy_e = x_dy[e]
            dh = nt(dy_e, w_down[l, e])
            u = u_s[l, e]
            t = jnp.tanh(TANH_A * (u + TANH_B * u * u * u))
            slope = 0.5 * (1.0 + t) + (0.5 * TANH_A) * u * (1.0 - t * t) * (1.0 + (3.0 * TANH_B) * u * u)
            du = (dh * slope).astype(BF16)
            x_du[e] = du
            x_hid[e] = (0.5 * u * (1.0 + t)).astype(BF16)
            y_s[e] = nt(du, w_up[l, e])
            return 0
        lax.fori_loop(0, local, expert, 0)
        send_a[l, 3] = join([y_s[e] for e in range(local)])
        exchange(3, l)

        def expert_grads(e, _):
            grads[l, 0, e] = tn(x_s[l, e], x_du[e]).astype(BF16)
            grads[l, 1, e] = tn(x_hid[e], x_dy[e]).astype(BF16)
            return 0
        lax.fori_loop(0, local, expert_grads, 0)

        @pl.when(p == l)
        def _():
            pltpu.make_async_copy(grads.at[l], own_out, gr_loc).start()

        @pl.when(p != l)
        def _():
            pltpu.make_async_remote_copy(
                src_ref=grads.at[l], dst_ref=recv_out, send_sem=gr_send, recv_sem=gr_recv,
                device_id={"pipe": other}, device_id_type=MESH).start()

        both = comb[l, 0:seq] + comb[l, seq:2 * seq]
        red_g[l, 0, :, :width] = nn(both, arrived(3, l).reshape(slots, width)).astype(BF16)
        reduce_start(red_g, (l,), 4 + l)
        h_mid = h_mid_s[l]
        scale = scale_of(h_mid)
        gain_two = gain[l, 1:2]
        summed = reduce_end(red_g, (l,), 4 + l)
        dn2 = summed[:, :width]
        tail = summed[:, width:]
        gg = [jnp.sum(jnp.where((at == kk) | (at == 2 + kk), tail, 0.0), -1, keepdims=True) for kk in range(2)]
        centre = gg[0] * gates[0] + gg[1] * gates[1]
        dprob = hot_e[0] * ((gg[0] - centre) / inv) + hot_e[1] * ((gg[1] - centre) / inv)
        dlog = (ep * (dprob - jnp.sum(ep * dprob, -1, keepdims=True))).astype(BF16)
        dn2 = dn2 + nt(jnp.concatenate([dlog, dlog], axis=1), router[l])
        small_g = tn(n_two[l], dlog)
        e33 = (at == 33).astype(F32).astype(BF16)
        small_g = small_g + tn((dn2 * h_mid * scale).astype(BF16), e33)
        dg = dn2 * gain_two
        dmid = g + scale * dg - h_mid * (scale * scale * scale) * jnp.mean(h_mid * dg, -1, keepdims=True)
        da = dmid.astype(BF16)
        chunk[l, :, 3] = tn(da, mixed_s[l]).astype(BF16).reshape(ne, rows, hw)
        dmixed = nt(da, w_out[l]).astype(BF16)
        q, k, v = qkv[l, 0], qkv[l, 1], qkv[l, 2]
        dq = jnp.zeros((seq, hw), F32)
        dk = jnp.zeros((seq, hw), F32)
        dv = jnp.zeros((seq, hw), F32)
        causal = lanes_of((seq, seq), 0) >= lanes_of((seq, seq), 1)
        row_at = lanes_of((seq, seq), 0)
        top = lanes_of((8, LANES), 0)
        bias_g = jnp.zeros((8, LANES), F32)
        for h in range(heads):
            mask = head_mask(h)
            prob = probs_s[l, h]
            dm = dmixed * mask
            dp = nt(dm, v)
            dv = dv + tn(prob.astype(BF16), dm)
            ds = jnp.where(causal, prob * (dp - jnp.sum(prob * dp, -1, keepdims=True)), 0.0).astype(BF16)
            dq = dq + nn(ds, k * mask)
            dk = dk + tn(ds, q * mask)
            turned = ds.astype(F32)
            bit = 1
            while bit < seq:
                turned = jnp.where((row_at & bit) != 0, pltpu.roll(turned, seq - bit, 1), turned)
                bit *= 2
            bias_g = bias_g + jnp.where(top == h, jnp.sum(turned, 0, keepdims=True), 0.0)
        dqkv[0] = (dq * (hd ** -0.5)).astype(BF16)
        dqkv[1] = (dk * (hd ** -0.5)).astype(BF16)
        dqkv[2] = dv.astype(BF16)
        dn1 = nt(dqkv[0], w_qkv[l, 0]) + nt(dqkv[1], w_qkv[l, 1]) + nt(dqkv[2], w_qkv[l, 2])
        red_a[l, 2, 0] = dn1.astype(BF16)
        reduce_start(red_a, (l, 2), 6 + l)
        n1 = n_one[l]
        for c in range(3):
            chunk[l, :, c] = tn(n1, dqkv[c]).astype(BF16).reshape(ne, rows, hw)

        def scatter(r, _):
            to = lax.rem(x + r, ne)
            pltpu.make_async_remote_copy(
                src_ref=chunk.at[l, to], dst_ref=chunk_in.at[l, r], send_sem=ck_send.at[l], recv_sem=ck_recv.at[l],
                device_id={"expert": to}, device_id_type=MESH).start()
            return 0
        lax.fori_loop(1, ne, scatter, 0)
        chunk_in[l, 0] = chunk[l, x]
        bias_high = bias_g.astype(BF16)
        bias_low = (bias_g - bias_high.astype(F32)).astype(BF16)
        bias_g = nn(bias_high, hot[...]) + nn(bias_low, hot[...])
        h_in = hs[l]
        scale_one = scale_of(h_in)
        dn1 = reduce_end(red_a, (l, 2), 6 + l)
        e32 = (at == 32).astype(F32).astype(BF16)
        small_g = small_g + tn((dn1 * h_in * scale_one).astype(BF16), e32)
        small_g = jnp.concatenate([small_g[:8] + bias_g, small_g[8:]], axis=0)
        small[l] = small_g.astype(BF16).reshape(ne, rows, LANES)

        def scatter_small(r, _):
            to = lax.rem(x + r, ne)
            pltpu.make_async_remote_copy(
                src_ref=small.at[l, to], dst_ref=small_in.at[l, r], send_sem=sm_send.at[l], recv_sem=sm_recv.at[l],
                device_id={"expert": to}, device_id_type=MESH).start()
            return 0
        lax.fori_loop(1, ne, scatter_small, 0)
        small_in[l, 0] = small[l, x]
        dg = dn1 * gain[l, 0:1]
        dh = dmid + scale_one * dg - h_in * (scale_one * scale_one * scale_one) * jnp.mean(h_in * dg, -1, keepdims=True)
        fin[...] = dh
        g_s[...] = dh.astype(BF16).astype(F32)
        return 0

    lax.fori_loop(0, 2, backward, 0)
    deliver(fin, 0)

    def settle(i, _):
        l = 1 - i
        for src, dst, send, recv, out, to, k in (
            (chunk, chunk_in, ck_send, ck_recv, shard, pair, 0),
            (small, small_in, sm_send, sm_recv, shard_small, pair_small, 1),
        ):
            part = src.at[l, pl.ds(1, ne - 1)]
            pltpu.make_async_copy(part, part, send.at[l]).wait()
            part = dst.at[l, pl.ds(1, ne - 1)]
            pltpu.make_async_copy(part, part, recv.at[l]).wait()
            acc = dst[l, 0].astype(F32)
            for r in range(1, ne):
                acc = acc + dst[l, r].astype(F32)
            out[l] = acc.astype(BF16)

            @pl.when(p != l)
            def _():
                pltpu.make_async_remote_copy(
                    src_ref=out.at[l], dst_ref=to, send_sem=pr_send.at[k], recv_sem=pr_recv.at[k],
                    device_id={"pipe": other}, device_id_type=MESH).start()
        return 0

    lax.fori_loop(0, 2, settle, 0)
    finals = ((shard, pair, total, attn_out, 0), (shard_small, pair_small, total_small, small_out, 1))
    for src, to, whole, dst, k in finals:
        pltpu.make_async_copy(to, to, pr_send.at[k]).wait()
        pltpu.make_async_copy(to, to, pr_recv.at[k]).wait()
        whole[...] = (src[p].astype(F32) + to[...].astype(F32)).astype(BF16)
        pltpu.make_async_copy(whole, dst.at[x], ag_loc.at[k]).start()

        def spread(r, _, whole=whole, dst=dst, k=k):
            pltpu.make_async_remote_copy(
                src_ref=whole, dst_ref=dst.at[x], send_sem=ag_send.at[k], recv_sem=ag_recv.at[k],
                device_id={"expert": lax.rem(x + r, ne)}, device_id_type=MESH).start()
            return 0
        lax.fori_loop(1, ne, spread, 0)

    for copy in outgoing:
        copy.wait_send()
    for sem in (gr_loc, gr_send, gr_recv):
        pltpu.make_async_copy(grads.at[0], grads.at[0], sem).wait()
    for sem in (sec_loc, sec_send, sec_recv):
        pltpu.make_async_copy(fin, fin, sem).wait()
    for src, to, whole, dst, k in finals:
        pltpu.make_async_copy(whole, whole, ag_loc.at[k]).wait()
        part = dst.at[pl.ds(0, ne - 1)]
        pltpu.make_async_copy(part, part, ag_send.at[k]).wait()
        pltpu.make_async_copy(part, part, ag_recv.at[k]).wait()


def body(
    block_input, cotangent, routes, offset_bucket, norm1_gain, qkv_weight, out_weight, bias_table, norm2_gain,
    router_weight, up_weight, down_weight,
):
    ne = lax.axis_size("expert")
    nz = lax.axis_size("tensor")
    micro, seq, width = block_input.shape
    heads, buckets = bias_table.shape[1:]
    local, _, ff = up_weight.shape[1:]
    hw = qkv_weight.shape[3]
    hd = hw // heads
    experts = router_weight.shape[2]
    rows = width // ne
    slots = ne * local * CAP

    routes_in = jnp.pad(routes[0], ((0, 0), (0, 0), (0, LANES - routes.shape[3])))
    back = jnp.roll(offset_bucket[::-1], 1)
    hot = (back[:, None] == jnp.arange(buckets, dtype=jnp.int32)[None, :]).astype(F32)
    hot_in = jnp.pad(hot, ((0, 0), (64, LANES - 64 - buckets))).astype(BF16)
    rel = jnp.sum(hot[None] * bias_table[0][:, None, :], -1)
    rel_in = jnp.pad(rel, ((0, 8 - heads), (0, 0)))
    gain_in = jnp.pad(jnp.concatenate([norm1_gain, norm2_gain], 0), ((0, 6), (0, 0)))
    high = lax.reduce_precision(router_weight[0], 8, 7)
    wide = ((0, 0), (0, LANES - experts))
    router_in = jnp.concatenate([jnp.pad(high, wide), jnp.pad(router_weight[0] - high, wide)], 1).astype(BF16)

    any_space = pl.BlockSpec(memory_space=pl.ANY)
    vm = pltpu.VMEM
    dma = pltpu.SemaphoreType.DMA
    sds = jax.ShapeDtypeStruct
    sec, own, recv, attn, small = pl.pallas_call(
        functools.partial(kernel, (ne, nz, seq, width, local, heads, ff, hd)),
        out_shape=[
            sds((micro, seq, width), F32), sds((2, local, width, ff), BF16), sds((2, local, width, ff), BF16),
            sds((ne, 4, rows, hw), BF16), sds((ne, rows, LANES), BF16),
        ],
        in_specs=[any_space] * 11,
        out_specs=[any_space] * 5,
        scratch_shapes=[
            vm((seq, width), BF16), vm((seq, width), BF16), vm((seq, LANES), BF16), vm((2, seq, LANES), jnp.int32),
            vm((2, 8, width), F32), vm((2, 8, LANES), F32), vm((2, width, 2 * LANES), BF16), vm((2, 3, width, hw), BF16),
            vm((2, hw, width), BF16), vm((2, local, width, ff), BF16), vm((2, local, ff, width), BF16),
            vm((3, seq, width), F32), vm((2, seq, width), BF16), vm((2, 3, seq, hw), BF16),
            vm((2, heads, seq, seq), F32), vm((2, seq, hw), BF16), vm((2, seq, width), F32), vm((2, seq, width), BF16),
            vm((2, 2 * seq, slots), BF16), vm((2, seq, LANES), F32), vm((2, local, ne * CAP, width), BF16),
            vm((2, local, ne * CAP, ff), F32), vm((local, ne * CAP, width), F32),
            vm((local, ne * CAP, width), BF16), vm((local, ne * CAP, ff), BF16), vm((local, ne * CAP, ff), BF16),
            vm((seq, width), F32), vm((seq, width), F32), vm((3, seq, hw), BF16),
            vm((2, 4, ne, 2 * CAP, width), BF16), vm((2, 4, ne, 2 * CAP, width), BF16),
            vm((2, 3, nz, seq, width), BF16), vm((2, nz, seq, width + LANES), BF16),
            vm((2, 2, local, width, ff), BF16), vm((2, ne, 4, rows, hw), BF16), vm((2, ne, 4, rows, hw), BF16),
            vm((2, ne, rows, LANES), BF16), vm((2, ne, rows, LANES), BF16),
            vm((2, 4, rows, hw), BF16), vm((2, rows, LANES), BF16), vm((4, rows, hw), BF16), vm((rows, LANES), BF16),
            vm((4, rows, hw), BF16), vm((rows, LANES), BF16),
            dma((3,)), dma((8, 2)), dma((8,)), dma((2, 4)), dma((2, 4)), dma((8,)), dma((8,)), dma, dma, dma,
            dma((2,)), dma((2,)), dma((2,)), dma((2,)), dma((2,)), dma((2,)), dma((2,)), dma((2,)), dma((2,)),
            dma, dma, dma,
        ],
        compiler_params=pltpu.CompilerParams(
            collective_id=0, has_side_effects=True, vmem_limit_bytes=60 * 1024 * 1024),
        cost_estimate=pl.CostEstimate(flops=20_000_000_000, bytes_accessed=40_000_000, transcendentals=2_000_000),
    )(
        block_input, cotangent, routes_in, hot_in, gain_in, rel_in, router_in, qkv_weight[0], out_weight[0],
        up_weight[0], down_weight[0],
    )
    both = own.astype(F32) + recv.astype(F32)
    attn = attn.transpose(1, 0, 2, 3).reshape(4, width, hw).astype(F32)
    small = small.reshape(width, LANES).astype(F32)
    return (
        sec[None], small[:, 32][None], attn[None, :3], attn[3].T[None], small[None, :heads, 64:64 + buckets],
        small[:, 33][None], small[None, :, :experts], both[None, 0], both[None, 1],
    )


def solution(mesh):
    in_specs = (
        P(None, "expert", None), P(None, "expert", None), P("pipe", None, "expert", None), P(), P("pipe", None),
        P("pipe", None, None, "tensor"), P("pipe", "tensor", None), P("pipe", "tensor", None), P("pipe", None),
        P("pipe", None, None), P("pipe", "expert", None, "tensor"), P("pipe", "expert", "tensor", None),
    )
    out_specs = (
        P("pipe", None, "expert", None), P("pipe", None), P("pipe", None, None, "tensor"), P("pipe", "tensor", None),
        P("pipe", "tensor", None), P("pipe", None), P("pipe", None, None), P("pipe", "expert", None, "tensor"),
        P("pipe", "expert", "tensor", None),
    )
    return jax.shard_map(body, mesh=mesh, in_specs=in_specs, out_specs=out_specs, check_vma=False)
```

time: 814 us -> 256 us (0.31); the launches traced: 801 us -> 255 us
  Pallas kernels: 0 us -> 220 us
  local copies, waits for them, and re-layouts: 186 us -> 25.1 us
  blocking collectives: 153 us -> 0 us
  other arithmetic: 134 us -> 9.08 us
  waiting for transfers between devices: 107 us -> 0 us
  matrix products: 105 us -> 0 us
  starting transfers between devices: 100 us -> 0 us
  between operations: 16.8 us -> 0.76 us
    pallas_call x0 -> x1, Pallas kernels: none -> 220 us  [body(): pl.pallas_call(functools.partial(kernel, (ne, nz, seq, width, local, head...]
    all_to_all x24 -> x0, waiting for transfers between devices: 105 us -> none  [the longest x6 24.6 us: summed_on_arrival(): lax.all_to_all(blocks, axis, split_axis=0, concat_axis=0, tiled=True)]
    dot_general x70 -> x0, matrix products: 102 us -> none  [the longest x12 19.4 us: gate_of(): logits = jnp.dot(normed, router, precision=lax.Precision.HIGHEST)]
    all_to_all x24 -> x0, starting transfers between devices: 99.9 us -> none  [the longest x6 27 us: copy_for_each(): return lax.all_to_all(copies, axis, split_axis=0, concat_axis=0, tiled=True)]
    all_gather x6 -> x0, blocking collectives: 77.5 us -> none  [the longest x3 39.3 us: layer_backward(): lax.all_gather(grad_back, 'tensor', axis=2, tiled=True)]
    psum x1 -> x0, blocking collectives: 75.4 us -> none  [body(): lax.psum(grad_table.astype(jnp.bfloat16), 'expert').astype(jnp.float32)]
    gather x8 -> x0, local copies, waits for them, and re-layouts: 73.6 us -> none  [the longest x2 61 us: body(): jnp.dot(bias_rows, bucket_hot.T, precision=lax.Precision.HIGHEST)]
    reduce_sum x57 -> x1, other arithmetic: 63.8 us -> 0.09 us  [body(): rel = jnp.sum(hot[None] * bias_table[0][:, None, :], -1)]
  transfers between devices with their start and end apart: 29 -> 0, of which waited for: 24 -> 0; matrix products, arithmetic and copies ran while one was open for 20% -> 0% of each run, Pallas kernels for 0% -> 0%
where the time goes in v1:
time: 256 us; the launch traced here: 255 us
  Pallas kernels  220 us (86%)
  local copies, waits for them, and re-layouts  25.1 us (10%)
  other arithmetic  9.08 us (4%)
    pallas_call x1, Pallas kernels, body(): pl.pallas_call(functools.partial(kernel, (ne, nz, seq, width, local, head...  220 us
    unnamed x15, local copies, waits for them, and re-layouts  12 us

profile of v1, /device:TPU:0, one launch (start us, length us, event | category | flops | bytes accessed | tf_op | source)
XLA Modules:
  0.0 254.8 jit_solution(6255266960453480468)
XLA Ops:
  0.7 1.1 copy.49
  1.8 0.8 fusion.3.router_in
  2.6 0.7 slice.39
  3.4 0.7 pad_add_fusion
  4.3 0.7 pad.27.hot_in
  5.0 0.7 copy.61
  5.8 0.6 pad.29.rel_in
  6.4 2.3 copy.50
  8.7 0.8 copy.46
  9.6 0.7 pad.26.routes_in
  10.2 0.6 select_maximum_fusion.gain_in
  10.8 219.8 %shard_map.187 = (f32[2,128,768]{2,1,0:T(8,128)}, bf16[2,2,768,768]{3,2,1,0:T(8,128)(2,1)}, bf16[2,2,768,768]{3,2,1,0:T(8,128)(2,1)}, bf16[16,4,48,192]{3,2,1,0:T(8,128)(2,1)}, bf16[16,48,128]{2,1,0:T(8,128)(2,1)}) custom-call(bf16[2,128,768]{2,1,0:T(8,128)(2,1)} %x_in.1, bf16[2,128,768]{2,1,0:T(8,128)(2,1)} %cot_in.1, s32[2,128,128]{2,1,0:T(8,128)} %pad.26.routes_in, ...), custom_call_target="tpu_custom_call" | custom-call | flops 20000000000 | bytes 40000000 | tf_op jit(solution)/shard_map/pallas_call | solution.py:479
  230.7 4.8 %convert_add_fusion = f32[2,2,768,768]{3,2,1,0:T(8,128)S(1)} fusion(bf16[2,2,768,768]{3,2,1,0:T(8,128)(2,1)} %get-tuple-element.18, bf16[2,2,768,768]{3,2,1,0:T(8,128)(2,1)} %get-tuple-element.17), kind=kLoop, calls=%fused_computation | loop fusion | flops 7077888 | bytes 18874368 | tf_op jit(solution)/shard_map/add | solution.py:514
  235.5 4.4 %fusion.6 = (f32[1,2,768,768]{3,2,1,0:T(8,128)}, f32[1,2,768,768]{3,2,1,0:T(8,128)}) fusion(f32[2,2,768,768]{3,2,1,0:T(8,128)S(1)} %convert_add_fusion), kind=kLoop, calls=%fused_computation.20 | loop fusion | bytes 18874368 | tf_op jit(solution)/shard_map/slice | solution.py:519
  240.2 0.6 broadcast_in_dim_squeeze.7
  240.9 0.6 copy.56
  241.5 0.8 copy.59
  242.4 0.7 copy.58
  243.1 1.8 convert_bitcast_fusion
  245.1 1.6 copy.51
  246.7 2.9 %copy.55 = f32[1,3,768,192]{2,3,1,0:T(8,128)} copy(f32[1,3,768,192]{3,2,1,0:T(8,128)} %bitcast.26) | data formatting | bytes 3538944
  249.6 1.0 slice.51
  250.5 2.2 copy.52
  252.7 2.1 copy.63
  (17 shorter events, 1.1 us)
Async XLA Ops:
  0.6 9.6 %copy-start.2 = (f32[1,768]{1,0:T(1,128)S(1)}, f32[1,768]{1,0:T(1,128)}, u32[]{:S(2)}) copy-start(f32[1,768]{1,0:T(1,128)} %param.16) | copy-start | bytes 9220
  0.7 9.6 %copy-start.1 = (f32[1,768]{1,0:T(1,128)S(1)}, f32[1,768]{1,0:T(1,128)}, u32[]{:S(2)}) copy-start(f32[1,768]{1,0:T(1,128)} %param.20) | copy-start | bytes 9220
  235.5 4.4 %copy-start = (bf16[16,48,128]{2,1,0:T(8,128)(2,1)S(1)}, bf16[16,48,128]{2,1,0:T(8,128)(2,1)}, u32[]{:S(2)}) copy-start(bf16[16,48,128]{2,1,0:T(8,128)(2,1)} %get-tuple-element.15) | copy-start | bytes 589828

commit v2 on v1

v2 whole, which is shorter than its diff:
```python
import functools

import jax
import jax.numpy as jnp
from jax import lax
from jax.experimental import pallas as pl
from jax.experimental.pallas import tpu as pltpu
from jax.sharding import PartitionSpec as P

EPS = 1e-06
MASKED = -1e30
MESH = pl.DeviceIdType.MESH
F32 = jnp.float32
BF16 = jnp.bfloat16
LANES = 128
CAP = 8
PARTS = 3
SMALL = 64
TANH_A = 0.7978845608
TANH_B = 0.044715


def dot(a, b, left, right):
    return lax.dot_general(a, b, (((left,), (right,)), ((), ())), preferred_element_type=F32)


def nn(a, b):
    return dot(a, b, 1, 0)


def nt(a, b):
    return dot(a, b, 1, 1)


def tn(a, b):
    return dot(a, b, 0, 0)


def lanes_of(shape, dim):
    return lax.broadcasted_iota(jnp.int32, shape, dim)


def kernel(
    dims,
    x_in, cot_in, routes_in, bucket_in, one_in, two_in, bias_in, router_in, qkv_in, out_in, up_in, down_in,
    sec_out, own_up, own_down, recv_up, recv_down, attn_out, small_out,
    xin, cot, bucket, hot, routes, gain_one, gain_two, bias_w, router, w_qkv, w_out, w_up, w_down,
    hs, n_one, qkv, probs_s, mixed_s, h_mid_s, n_two, comb, eprobs, x_s, u_s, x_dy, x_du, x_hid, g_s, fin, dqkv,
    send_a, recv_a, send_c, recv_c, red_a, red_c, red_g, g_up, g_down, chunk, chunk_pair, chunk_in, flat, small, small_pair,
    small_in, total, total_small,
    sem_in, sem_w, sem_ws, sa_send, sa_recv, sc_send, sc_recv, rd_send, rd_recv, rc_send, rc_recv, gr_send, gr_recv, gr_loc,
    ck_send, ck_recv, pr_send, pr_recv, ag_send, ag_recv, ag_loc, sec_send, sec_recv, sec_loc,
):
    ne, nz, seq, width, local, heads, ff, hd = dims
    p = lax.axis_index("pipe")
    x = lax.axis_index("expert")
    z = lax.axis_index("tensor")
    other = 1 - p
    slots = ne * 2 * CAP
    hw = heads * hd
    rows = width // ne
    parts_c = PARTS
    part_w = width // parts_c
    fold = width // LANES
    per = hw // rows
    flat_rows = fold * SMALL // ne

    barrier = pltpu.get_barrier_semaphore()

    def hello_e(r, _):
        pl.semaphore_signal(barrier, inc=1, device_id={"expert": lax.rem(x + r, ne)}, device_id_type=MESH)
        return 0

    def hello_z(r, _):
        pl.semaphore_signal(barrier, inc=1, device_id={"tensor": lax.rem(z + r, nz)}, device_id_type=MESH)
        return 0

    lax.fori_loop(1, ne, hello_e, 0)
    lax.fori_loop(1, nz, hello_z, 0)
    pl.semaphore_signal(barrier, inc=1, device_id={"pipe": other}, device_id_type=MESH)

    ins = [
        pltpu.make_async_copy(x_in.at[p], xin, sem_in.at[0]),
        pltpu.make_async_copy(cot_in.at[p], cot, sem_in.at[1]),
        pltpu.make_async_copy(bucket_in, bucket, sem_in.at[2]),
    ]
    for copy in ins:
        copy.start()
    weights = [
        (one_in, gain_one), (qkv_in, w_qkv), (bias_in, bias_w), (out_in, w_out), (routes_in, routes), (router_in, router),
        (two_in, gain_two), (up_in, w_up), (down_in, w_down),
    ]
    for k, (src, dst) in enumerate(weights):
        pltpu.make_async_copy(src.at[p] if k == 4 else src, dst.at[p], sem_w.at[k, p]).start()
    pl.semaphore_wait(barrier, ne - 1 + nz - 1 + 1)
    outgoing = []
    for k, (src, dst) in enumerate(weights):
        copy = pltpu.make_async_remote_copy(
            src_ref=src.at[other] if k == 4 else src, dst_ref=dst.at[p], send_sem=sem_ws.at[k], recv_sem=sem_w.at[k, p],
            device_id={"pipe": other}, device_id_type=MESH)
        copy.start()
        outgoing.append(copy)

    def await_weight(k, l):
        dst = weights[k][1]
        pltpu.make_async_copy(dst.at[l], dst.at[l], sem_w.at[k, l]).wait()

    def send_all(src, dst, send, recv, forth):
        def one(r, _):
            pltpu.make_async_remote_copy(
                src_ref=src.at[r], dst_ref=dst.at[r], send_sem=send, recv_sem=recv,
                device_id={"expert": lax.rem(x + r if forth else x + ne - r, ne)}, device_id_type=MESH).start()
            return 0
        lax.fori_loop(1, ne, one, 0)
        dst[0] = src[0]

    def await_all(src, dst, send, recv):
        part = src.at[pl.ds(1, ne - 1)]
        pltpu.make_async_copy(part, part, send).wait()
        part = dst.at[pl.ds(1, ne - 1)]
        pltpu.make_async_copy(part, part, recv).wait()

    def exchange(kind, l):
        send_all(send_a.at[l, kind], recv_a.at[l, kind], sa_send.at[l, kind], sa_recv.at[l, kind], True)

    def arrived(kind, l):
        await_all(send_a.at[l, kind], recv_a.at[l, kind], sa_send.at[l, kind], sa_recv.at[l, kind])
        return recv_a[l, kind]

    def exchange_back(kind, l, c):
        send_all(send_c.at[l, kind, c], recv_c.at[l, kind, c], sc_send.at[l, kind, c], sc_recv.at[l, kind, c], False)

    def arrived_back(kind, l, c):
        await_all(send_c.at[l, kind, c], recv_c.at[l, kind, c], sc_send.at[l, kind, c], sc_recv.at[l, kind, c])
        return recv_c[l, kind, c].reshape(slots, part_w)

    def reduce_start(buf, send, recv):
        def one(r, _):
            pltpu.make_async_remote_copy(
                src_ref=buf.at[0], dst_ref=buf.at[r], send_sem=send, recv_sem=recv,
                device_id={"tensor": lax.rem(z + r, nz)}, device_id_type=MESH).start()
            return 0
        lax.fori_loop(1, nz, one, 0)

    def reduce_end(buf, send, recv):
        part = buf.at[pl.ds(1, nz - 1)]
        pltpu.make_async_copy(part, part, send).wait()
        pltpu.make_async_copy(part, part, recv).wait()
        acc = None
        for a in range(nz):
            term = buf[lax.rem(z + nz - a, nz)].astype(F32)
            acc = term if acc is None else acc + term
        return acc

    def summed_back(kind, l, weigh):
        for c in range(parts_c):
            red_c[l, kind, c, 0] = weigh(arrived_back(kind, l, c)).astype(BF16)
            reduce_start(red_c.at[l, kind, c], rc_send.at[l, kind, c], rc_recv.at[l, kind, c])
        return lambda: jnp.concatenate(
            [reduce_end(red_c.at[l, kind, c], rc_send.at[l, kind, c], rc_recv.at[l, kind, c]) for c in range(parts_c)], axis=1)

    def split(blocks):
        wide = blocks.astype(F32)
        return [wide[:, e * CAP:(e + 1) * CAP].reshape(ne * CAP, width).astype(BF16) for e in range(local)]

    def join(parts):
        return jnp.concatenate([part.reshape(ne, CAP, part_w) for part in parts], axis=1).astype(BF16)

    def head_mask(h):
        at = lanes_of((1, hw), 1)
        return ((at >= h * hd) & (at < (h + 1) * hd)).astype(BF16)

    def scale_of(h):
        return lax.rsqrt(jnp.mean(h * h, -1, keepdims=True) + EPS)

    def column(row):
        eye = lanes_of((seq, seq), 0) == lanes_of((seq, seq), 1)
        return jnp.sum(jnp.where(eye, row.astype(F32), 0.0), -1, keepdims=True)

    def chosen_of(ids):
        at = lanes_of((seq, ne * local), 1)
        return [(at == e).astype(F32) for e in ids]

    def named(l):
        return [column(routes[l, k:k + 1]).astype(jnp.int32) for k in range(2)]

    def router_of(l):
        r = router[l]
        high = r.astype(BF16)
        return high, (r - high.astype(F32)).astype(BF16)

    def forward(l, _):
        h_in = hs[l]
        await_weight(0, l)
        n1 = (h_in * scale_of(h_in) * gain_one[l]).astype(BF16)
        n_one[l] = n1
        await_weight(1, l)
        for c in range(3):
            qkv[l, c] = nt(n1, w_qkv[l, c]).astype(BF16)
        q, k, v = qkv[l, 0], qkv[l, 1], qkv[l, 2]
        await_weight(2, l)
        causal = lanes_of((seq, seq), 0) >= lanes_of((seq, seq), 1)
        mixed = jnp.zeros((seq, hw), F32)
        for h in range(heads):
            mask = head_mask(h)
            rel = lax.dot_general(
                jnp.broadcast_to(bias_w[l, h], (8, hot.shape[1])), hot[...], (((1,), (1,)), ((), ())),
                precision=lax.Precision.HIGHEST, preferred_element_type=F32)
            bias = pltpu.roll(jnp.broadcast_to(rel[0:1], (seq, seq)), 0, 1, stride=1, stride_axis=0)
            s = nt(q * mask, k) * (hd ** -0.5) + bias
            s = jnp.where(causal, s, MASKED)
            e = jnp.exp(s - jnp.max(s, -1, keepdims=True))
            prob = e / jnp.sum(e, -1, keepdims=True)
            probs_s[l, h] = prob
            mixed = mixed + nn(prob.astype(BF16), v * mask)
        mixed = mixed.astype(BF16)
        mixed_s[l] = mixed
        await_weight(3, l)
        red_a[l, 0, 0] = nn(mixed, w_out[l]).astype(BF16)
        reduce_start(red_a.at[l, 0], rd_send.at[l, 0], rd_recv.at[l, 0])

        await_weight(4, l)
        ids = named(l)
        hot_e = chosen_of(ids)
        row_at, col_at = lanes_of((seq, seq), 0), lanes_of((seq, seq), 1)
        earlier = (row_at > col_at).astype(BF16)
        count = nn(earlier, (hot_e[0] + hot_e[1]).astype(BF16))
        for kk in range(2):
            before = count if kk == 0 else count + hot_e[0]
            c = jnp.sum(before * hot_e[kk], -1, keepdims=True).astype(jnp.int32)
            e = ids[kk]
            place = (((e >> 1) - x + ne) & (ne - 1)) * (2 * CAP) + (e & 1) * CAP + c
            comb[l, kk * seq:(kk + 1) * seq] = (lanes_of((seq, slots), 1) == place).astype(F32).astype(BF16)
        both = comb[l, 0:seq] + comb[l, seq:2 * seq]
        await_weight(5, l)
        await_weight(6, l)

        h_mid = h_in + reduce_end(red_a.at[l, 0], rd_send.at[l, 0], rd_recv.at[l, 0])
        h_mid_s[l] = h_mid
        n2 = (h_mid * scale_of(h_mid) * gain_two[l]).astype(BF16)
        n_two[l] = n2
        send_a[l, 0] = tn(both, n2).astype(BF16).reshape(ne, 2 * CAP, width)
        exchange(0, l)
        high, low = router_of(l)
        logits = nt(n2, high) + nt(n2, low)
        e = jnp.exp(logits - jnp.max(logits, -1, keepdims=True))
        ep = e / jnp.sum(e, -1, keepdims=True)
        eprobs[l] = ep
        picked = [jnp.sum(ep * hot_e[kk], -1, keepdims=True) for kk in range(2)]
        inv = picked[0] + picked[1]
        gates = [picked[kk] / inv for kk in range(2)]
        await_weight(7, l)
        await_weight(8, l)
        parts = split(arrived(0, l))
        for e in range(local):
            x_s[l, e] = parts[e]

        def expert(e, _):
            u = nn(x_s[l, e], w_up[l, e])
            u_s[l, e] = u
            t = jnp.tanh(TANH_A * (u + TANH_B * u * u * u))
            x_hid[e] = (0.5 * u * (1.0 + t)).astype(BF16)
            return 0
        lax.fori_loop(0, local, expert, 0)
        for c in range(parts_c):
            cols = slice(c * part_w, (c + 1) * part_w)
            send_c[l, 0, c] = join([nn(x_hid[e], w_down[l, e, :, cols]) for e in range(local)])
            exchange_back(0, l, c)
        out = summed_back(0, l, lambda back: gates[0] * nn(comb[l, 0:seq], back) + gates[1] * nn(comb[l, seq:2 * seq], back))
        out = h_mid + out()
        hs[l + 1] = jnp.where(l == 0, out.astype(BF16).astype(F32), out)
        return 0

    for copy in ins:
        copy.wait()
    hs[0] = xin[...].astype(F32)
    turn_at, turn_of = lanes_of((seq, seq), 0), lanes_of((seq, seq), 1)
    turned_bucket = jnp.where((turn_at + turn_of == 0) | (turn_at + turn_of == seq), bucket[...].astype(F32), 0.0)
    turned_bucket = jnp.sum(turned_bucket, -1, keepdims=True).astype(jnp.int32)
    hot[...] = (turned_bucket == lanes_of(hot.shape, 1)).astype(F32)
    lax.fori_loop(0, 2, forward, 0)

    def deliver(src, owner):
        @pl.when(p == owner)
        def _():
            pltpu.make_async_copy(src, sec_out.at[p], sec_loc).start()

        @pl.when(p != owner)
        def _():
            pltpu.make_async_remote_copy(
                src_ref=src, dst_ref=sec_out.at[p], send_sem=sec_send, recv_sem=sec_recv,
                device_id={"pipe": other}, device_id_type=MESH).start()

    def merge(k, src, pair, mine, within, dst, send, recv):
        pltpu.make_async_copy(pair, pair, pr_recv.at[k]).wait()
        mine[...] = (src[p].astype(F32) + pair[...].astype(F32)).astype(mine.dtype)

        def scatter(r, _):
            to = lax.rem(x + r, ne)
            pltpu.make_async_remote_copy(
                src_ref=within(mine, to), dst_ref=dst.at[r], send_sem=send, recv_sem=recv,
                device_id={"expert": to}, device_id_type=MESH).start()
            return 0
        lax.fori_loop(1, ne, scatter, 0)

    def merge_attn():
        merge(0, chunk, chunk_pair, chunk_pair, lambda ref, j: ref.at[j], chunk_in, ck_send.at[0], ck_recv.at[0])
        chunk_in[0] = chunk_pair[x]

    def piece(ref, j):
        return ref.at[pl.ds(pl.multiple_of(j * flat_rows, 8), flat_rows)]

    def merge_small():
        merge(1, small, small_pair, small_pair, piece, small_in, ck_send.at[1], ck_recv.at[1])
        small_in[0] = small_pair[pl.ds(pl.multiple_of(x * flat_rows, 8), flat_rows)]

    def spread(k, arrived_at, whole, dst):
        part = arrived_at.at[pl.ds(1, ne - 1)]
        pltpu.make_async_copy(part, part, ck_send.at[k]).wait()
        pltpu.make_async_copy(part, part, ck_recv.at[k]).wait()
        acc = arrived_at[0].astype(F32)
        for r in range(1, ne):
            acc = acc + arrived_at[r].astype(F32)
        whole[...] = acc.astype(whole.dtype)
        pltpu.make_async_copy(whole, dst, ag_loc.at[k]).start()

        def one(r, _):
            pltpu.make_async_remote_copy(
                src_ref=whole, dst_ref=dst, send_sem=ag_send.at[k], recv_sem=ag_recv.at[k],
                device_id={"expert": lax.rem(x + r, ne)}, device_id_type=MESH).start()
            return 0
        lax.fori_loop(1, ne, one, 0)

    def spread_attn():
        spread(0, chunk_in, total, attn_out.at[x])

    def spread_small():
        spread(1, small_in, total_small, piece(small_out, x))

    def to_partner(src, dst, send, recv):
        pltpu.make_async_remote_copy(
            src_ref=src, dst_ref=dst, send_sem=send, recv_sem=recv, device_id={"pipe": other}, device_id_type=MESH).start()

    deliver(hs.at[2], 1)
    g_s[...] = cot[...].astype(F32)

    def backward(i, _):
        l = 1 - i
        g = g_s[...]
        hot_e = chosen_of(named(l))
        ep = eprobs[l]
        picked = [jnp.sum(ep * hot_e[kk], -1, keepdims=True) for kk in range(2)]
        inv = picked[0] + picked[1]
        gates = [picked[kk] / inv for kk in range(2)]
        dy = jnp.concatenate([(gates[kk] * g).astype(BF16) for kk in range(2)], axis=0)
        send_a[l, 1] = tn(comb[l], dy).astype(BF16).reshape(ne, 2 * CAP, width)
        exchange(1, l)

        @pl.when((p == 1) & (l == 0))
        def _():
            merge_attn()
            merge_small()

        at = lanes_of((seq, LANES), 1)
        gg = jnp.zeros((seq, LANES), F32)
        for kk in range(2):
            part = None
            for c in range(parts_c):
                got = nn(comb[l, kk * seq:(kk + 1) * seq], recv_c[l, 0, c].reshape(slots, part_w))
                term = jnp.sum(g[:, c * part_w:(c + 1) * part_w] * got, -1, keepdims=True)
                part = term if part is None else part + term
            high = part.astype(BF16).astype(F32)
            gg = gg + jnp.where(at == kk, high, 0.0) + jnp.where(at == 2 + kk, part - high, 0.0)
        red_g[l, 0] = gg.astype(BF16)
        reduce_start(red_g.at[l], rd_send.at[l, 2], rd_recv.at[l, 2])
        parts = split(arrived(1, l))
        for e in range(local):
            x_dy[e] = parts[e]

        def expert(e, _):
            dy_e = x_dy[e]
            dh = nt(dy_e, w_down[l, e])
            u = u_s[l, e]
            t = jnp.tanh(TANH_A * (u + TANH_B * u * u * u))
            slope = 0.5 * (1.0 + t) + (0.5 * TANH_A) * u * (1.0 - t * t) * (1.0 + (3.0 * TANH_B) * u * u)
            du = (dh * slope).astype(BF16)
            x_du[e] = du
            x_hid[e] = (0.5 * u * (1.0 + t)).astype(BF16)
            return 0
        lax.fori_loop(0, local, expert, 0)
        for c in range(parts_c):
            cols = slice(c * part_w, (c + 1) * part_w)
            send_c[l, 1, c] = join([nt(x_du[e], w_up[l, e, cols]) for e in range(local)])
            exchange_back(1, l, c)

        @pl.when((p == 1) & (l == 0))
        def _():
            spread_attn()
            spread_small()

        def expert_grads(e, _):
            g_up[l, e] = tn(x_s[l, e], x_du[e]).astype(BF16)
            g_down[l, e] = tn(x_hid[e], x_dy[e]).astype(BF16)
            return 0
        lax.fori_loop(0, local, expert_grads, 0)

        both = comb[l, 0:seq] + comb[l, seq:2 * seq]
        dn2 = summed_back(1, l, lambda back: nn(both, back))

        @pl.when(p == l)
        def _():
            pltpu.make_async_copy(g_up.at[l], own_up, gr_loc.at[0]).start()
            pltpu.make_async_copy(g_down.at[l], own_down, gr_loc.at[1]).start()

        @pl.when(p != l)
        def _():
            to_partner(g_up.at[l], recv_up, gr_send.at[0], gr_recv.at[0])
            to_partner(g_down.at[l], recv_down, gr_send.at[1], gr_recv.at[1])

        h_mid = h_mid_s[l]
        scale = scale_of(h_mid)
        tail = reduce_end(red_g.at[l], rd_send.at[l, 2], rd_recv.at[l, 2])
        dn2 = dn2()
        gg = [jnp.sum(jnp.where((at == kk) | (at == 2 + kk), tail, 0.0), -1, keepdims=True) for kk in range(2)]
        centre = gg[0] * gates[0] + gg[1] * gates[1]
        dprob = hot_e[0] * ((gg[0] - centre) / inv) + hot_e[1] * ((gg[1] - centre) / inv)
        dlog = (ep * (dprob - jnp.sum(ep * dprob, -1, keepdims=True))).astype(BF16)
        high, low = router_of(l)
        dn2 = dn2 + nn(dlog, high) + nn(dlog, low)
        flat[...] = jnp.zeros_like(flat)
        flat[0:ne * local] = tn(dlog, n_two[l])
        flat[ne * local + 1:ne * local + 2] = jnp.sum(dn2 * h_mid * scale, 0, keepdims=True)
        dg = dn2 * gain_two[l]
        dmid = g + scale * dg - h_mid * (scale * scale * scale) * jnp.mean(h_mid * dg, -1, keepdims=True)
        da = dmid.astype(BF16)
        chunk[l, 3 * per:4 * per] = tn(mixed_s[l], da).astype(BF16).reshape(per, rows, width)
        dmixed = nt(da, w_out[l]).astype(BF16)
        q, k, v = qkv[l, 0], qkv[l, 1], qkv[l, 2]
        dq = jnp.zeros((seq, hw), F32)
        dk = jnp.zeros((seq, hw), F32)
        dv = jnp.zeros((seq, hw), F32)
        causal = lanes_of((seq, seq), 0) >= lanes_of((seq, seq), 1)
        row_at = lanes_of((seq, seq), 0)
        top = lanes_of((8, LANES), 0)
        bias_g = jnp.zeros((8, LANES), F32)
        for h in range(heads):
            mask = head_mask(h)
            prob = probs_s[l, h]
            dm = dmixed * mask
            dp = nt(dm, v)
            dv = dv + tn(prob.astype(BF16), dm)
            ds = jnp.where(causal, prob * (dp - jnp.sum(prob * dp, -1, keepdims=True)), 0.0).astype(BF16)
            dq = dq + nn(ds, k * mask)
            dk = dk + tn(ds, q * mask)
            turned = ds.astype(F32)
            bit = 1
            while bit < seq:
                turned = jnp.where((row_at & bit) != 0, pltpu.roll(turned, seq - bit, 1), turned)
                bit *= 2
            bias_g = bias_g + jnp.where(top == h, jnp.sum(turned, 0, keepdims=True), 0.0)
        dqkv[0] = (dq * (hd ** -0.5)).astype(BF16)
        dqkv[1] = (dk * (hd ** -0.5)).astype(BF16)
        dqkv[2] = dv.astype(BF16)
        dn1 = nn(dqkv[0], w_qkv[l, 0]) + nn(dqkv[1], w_qkv[l, 1]) + nn(dqkv[2], w_qkv[l, 2])
        red_a[l, 1, 0] = dn1.astype(BF16)
        reduce_start(red_a.at[l, 1], rd_send.at[l, 1], rd_recv.at[l, 1])
        n1 = n_one[l]
        for c in range(3):
            chunk[l, c * per:(c + 1) * per] = tn(dqkv[c], n1).astype(BF16).reshape(per, rows, width)

        @pl.when(p != l)
        def _():
            to_partner(chunk.at[l], chunk_pair, pr_send.at[0], pr_recv.at[0])

        @pl.when((p == 0) & (l == 0))
        def _():
            merge_attn()

        bias_high = bias_g.astype(BF16)
        bias_low = (bias_g - bias_high.astype(F32)).astype(BF16)
        hot_b = hot[...].astype(BF16)
        flat[ne * local + 8:ne * local + 16, 0:hot.shape[1]] = nn(bias_high, hot_b) + nn(bias_low, hot_b)
        h_in = hs[l]
        scale_one = scale_of(h_in)
        dn1 = reduce_end(red_a.at[l, 1], rd_send.at[l, 1], rd_recv.at[l, 1])
        flat[ne * local:ne * local + 1] = jnp.sum(dn1 * h_in * scale_one, 0, keepdims=True)
        for b in range(fold):
            small[l, b * SMALL:(b + 1) * SMALL] = flat[:, b * LANES:(b + 1) * LANES]

        @pl.when(p != l)
        def _():
            to_partner(small.at[l], small_pair, pr_send.at[1], pr_recv.at[1])

        dg = dn1 * gain_one[l]
        dh = dmid + scale_one * dg - h_in * (scale_one * scale_one * scale_one) * jnp.mean(h_in * dg, -1, keepdims=True)
        fin[...] = dh
        g_s[...] = dh.astype(BF16).astype(F32)
        return 0

    lax.fori_loop(0, 2, backward, 0)
    deliver(fin, 0)

    @pl.when(p == 0)
    def _():
        merge_small()
        spread_attn()
        spread_small()

    for copy in outgoing:
        copy.wait_send()
    for k, ref in enumerate((g_up, g_down)):
        for sem in (gr_loc, gr_send, gr_recv):
            pltpu.make_async_copy(ref.at[0], ref.at[0], sem.at[k]).wait()
    for sem in (sec_loc, sec_send, sec_recv):
        pltpu.make_async_copy(fin, fin, sem).wait()
    for k, (pair, whole, arrived_at) in enumerate(((chunk_pair, total, chunk_in), (small_pair, total_small, small_in))):
        pltpu.make_async_copy(pair, pair, pr_send.at[k]).wait()
        pltpu.make_async_copy(whole, whole, ag_loc.at[k]).wait()
        part = arrived_at.at[pl.ds(1, ne - 1)]
        pltpu.make_async_copy(part, part, ag_send.at[k]).wait()
        pltpu.make_async_copy(part, part, ag_recv.at[k]).wait()


def body(
    block_input, cotangent, routes, offset_bucket, norm1_gain, qkv_weight, out_weight, bias_table, norm2_gain,
    router_weight, up_weight, down_weight,
):
    ne = lax.axis_size("expert")
    nz = lax.axis_size("tensor")
    micro, seq, width = block_input.shape
    heads, buckets = bias_table.shape[1:]
    local, _, ff = up_weight.shape[1:]
    hw = qkv_weight.shape[3]
    hd = hw // heads
    experts = router_weight.shape[2]
    rows = width // ne
    parts_c = PARTS
    part_w = width // parts_c
    fold = width // LANES
    per = hw // rows
    flat_rows = fold * SMALL // ne
    slots = ne * local * CAP

    any_space = pl.BlockSpec(memory_space=pl.ANY)
    vm = pltpu.VMEM
    dma = pltpu.SemaphoreType.DMA
    sds = jax.ShapeDtypeStruct
    part_w = width // PARTS
    flat = width // LANES * SMALL
    parts_in = (2, 2, PARTS, ne, 2 * CAP, part_w)
    half = (local, width, ff)
    sec, own_up, own_down, recv_up, recv_down, attn, small = pl.pallas_call(
        functools.partial(kernel, (ne, nz, seq, width, local, heads, ff, hd)),
        out_shape=[
            sds((micro, seq, width), F32), sds(half, BF16), sds(half, BF16), sds(half, BF16), sds(half, BF16),
            sds((ne, rows, width), BF16), sds((flat, LANES), F32),
        ],
        in_specs=[any_space] * 12,
        out_specs=[any_space] * 7,
        scratch_shapes=[
            vm((seq, width), BF16), vm((seq, width), BF16), vm((1, seq), jnp.int32), vm((seq, buckets), F32),
            vm((2, 2, seq), jnp.int32), vm((2, 1, width), F32), vm((2, 1, width), F32), vm((2, heads, 1, buckets), F32),
            vm((2, experts, width), F32), vm((2, 3, hw, width), BF16),
            vm((2, hw, width), BF16), vm((2, local, width, ff), BF16), vm((2, local, ff, width), BF16),
            vm((3, seq, width), F32), vm((2, seq, width), BF16), vm((2, 3, seq, hw), BF16),
            vm((2, heads, seq, seq), F32), vm((2, seq, hw), BF16), vm((2, seq, width), F32), vm((2, seq, width), BF16),
            vm((2, 2 * seq, slots), BF16), vm((2, seq, experts), F32), vm((2, local, ne * CAP, width), BF16),
            vm((2, local, ne * CAP, ff), F32),
            vm((local, ne * CAP, width), BF16), vm((local, ne * CAP, ff), BF16), vm((local, ne * CAP, ff), BF16),
            vm((seq, width), F32), vm((seq, width), F32), vm((3, seq, hw), BF16),
            vm((2, 2, ne, 2 * CAP, width), BF16), vm((2, 2, ne, 2 * CAP, width), BF16), vm(parts_in, BF16), vm(parts_in, BF16),
            vm((2, 2, nz, seq, width), BF16), vm((2, 2, PARTS, nz, seq, part_w), BF16), vm((2, nz, seq, LANES), BF16),
            vm((2, *half), BF16), vm((2, *half), BF16), vm((2, ne, rows, width), BF16), vm((ne, rows, width), BF16),
            vm((ne, rows, width), BF16), vm((SMALL, width), F32), vm((2, flat, LANES), F32), vm((flat, LANES), F32),
            vm((ne, flat // ne, LANES), F32), vm((rows, width), BF16), vm((flat // ne, LANES), F32),
            dma((3,)), dma((9, 2)), dma((9,)), dma((2, 2)), dma((2, 2)), dma((2, 2, PARTS)), dma((2, 2, PARTS)),
            dma((2, 3)), dma((2, 3)), dma((2, 2, PARTS)), dma((2, 2, PARTS)), dma((2,)), dma((2,)), dma((2,)),
            dma((2,)), dma((2,)), dma((2,)), dma((2,)), dma((2,)), dma((2,)), dma((2,)), dma, dma, dma,
        ],
        compiler_params=pltpu.CompilerParams(
            collective_id=0, has_side_effects=True, vmem_limit_bytes=60 * 1024 * 1024),
        cost_estimate=pl.CostEstimate(flops=20_000_000_000, bytes_accessed=40_000_000, transcendentals=2_000_000),
    )(
        block_input, cotangent, routes[0].transpose(0, 2, 1), offset_bucket[None], norm1_gain, norm2_gain,
        bias_table.transpose(1, 0, 2), router_weight[0].T, qkv_weight[0].transpose(0, 2, 1), out_weight[0],
        up_weight[0], down_weight[0],
    )
    grad_up = own_up.astype(F32) + recv_up.astype(F32)
    grad_down = own_down.astype(F32) + recv_down.astype(F32)
    attn = attn.reshape(4, hw, width).astype(F32)
    small = small.reshape(width // LANES, SMALL, LANES).transpose(1, 0, 2).reshape(SMALL, width)
    return (
        sec[None], small[experts][None], attn[None, :3].transpose(0, 1, 3, 2), attn[3][None],
        small[None, experts + 8:experts + 8 + heads, :buckets], small[experts + 1][None], small[:experts].T[None],
        grad_up[None], grad_down[None],
    )


def solution(mesh):
    in_specs = (
        P(None, "expert", None), P(None, "expert", None), P("pipe", None, "expert", None), P(), P("pipe", None),
        P("pipe", None, None, "tensor"), P("pipe", "tensor", None), P("pipe", "tensor", None), P("pipe", None),
        P("pipe", None, None), P("pipe", "expert", None, "tensor"), P("pipe", "expert", "tensor", None),
    )
    out_specs = (
        P("pipe", None, "expert", None), P("pipe", None), P("pipe", None, None, "tensor"), P("pipe", "tensor", None),
        P("pipe", "tensor", None), P("pipe", None), P("pipe", None, None), P("pipe", "expert", None, "tensor"),
        P("pipe", "expert", "tensor", None),
    )
    return jax.shard_map(body, mesh=mesh, in_specs=in_specs, out_specs=out_specs, check_vma=False)
```

time: 256 us -> 190 us (0.74)
  Pallas kernels: 220 us -> 176 us
  local copies, waits for them, and re-layouts: 25.1 us -> 5.12 us
    pallas_call x1, Pallas kernels: 220 us -> 176 us  [body(): pl.pallas_call(functools.partial(kernel, (ne, nz, seq, width, local, head...]
    unnamed x15 -> x11, local copies, waits for them, and re-layouts: 12 us -> 2.16 us
    broadcast_in_dim x0 -> x1, other arithmetic: none -> 8.65 us  [body(): grad_down[None]]
    slice x9 -> x4, local copies, waits for them, and re-layouts: 8.29 us -> 2.83 us  [the longest x1 1.38 us: body(): attn[None, :3].transpose(0, 1, 3, 2)]
    add x1 -> x0, other arithmetic: 4.82 us -> none  [body(): both = own.astype(F32) + recv.astype(F32)]
where the time goes in v2:
time: 190 us
  Pallas kernels  176 us (93%)
  other arithmetic  8.65 us (5%)
  local copies, waits for them, and re-layouts  5.12 us (3%)
    pallas_call x1, Pallas kernels, body(): pl.pallas_call(functools.partial(kernel, (ne, nz, seq, width, local, head...  176 us
    broadcast_in_dim x1, other arithmetic, body(): grad_down[None]  8.65 us

profile of v2, /device:TPU:0, one launch (start us, length us, event | category | flops | bytes accessed | tf_op | source)
XLA Modules:
  0.0 190.2 jit_solution(17243392015631458010)
XLA Ops:
  0.6 175.7 %shard_map.187 = (f32[2,128,768]{2,1,0:T(8,128)}, bf16[2,768,768]{2,1,0:T(8,128)(2,1)}, bf16[2,768,768]{2,1,0:T(8,128)(2,1)}, bf16[2,768,768]{2,1,0:T(8,128)(2,1...) custom-call(bf16[2,128,768]{2,1,0:T(8,128)(2,1)} %x_in.1, ...), custom_call_target="tpu_custom_call" | custom-call | flops 20000000000 | bytes 40000000 | tf_op jit(solution)/shard_map/pallas_call | solution.py:552
  176.4 0.0 copy-start.2
  176.4 0.0 copy-start
  176.4 8.7 %add_bitcast_fusion = (f32[1,2,768,768]{3,2,1,0:T(8,128)}, f32[1,2,768,768]{3,2,1,0:T(8,128)}) fusion(bf16[2,768,768]{2,1,0:T(8,128)(2,1)} %get-tuple-element.22, bf16[2,768,768]{2,1,0:T(8,128)(2,1)} %get-tuple-element.21, bf16[2,768,768]{2,1,0:T(8,128)(2,1)} %get-tuple-element.20, bf16[2,768,768]{2,1,0:T(8,128)(2,1)} %get-tuple-element.19), kind=kLoop, calls=%fused_computation | loop fusion | flops 7077888 | bytes 18874368 | tf_op jit(solution)/shard_map/broadcast_in_dim | solution.py:595
  185.1 0.0 copy-done.2
  185.1 0.1 copy.40
  185.2 0.6 copy_bitcast_fusion.2
  185.8 0.7 copy.39
  186.5 0.0 copy-done
  186.5 0.0 copy-start.1
  186.5 1.4 slice.42
  187.9 0.9 slice.43
  188.8 0.6 copy.27
  189.3 0.0 copy-done.1
  189.3 0.9 copy.42
  (4 shorter events, 0.1 us)
Async XLA Ops:
  176.4 8.7 %copy-start.2 = (f32[384,128]{1,0:T(8,128)S(1)}, f32[384,128]{1,0:T(8,128)}, u32[]{:S(2)}) copy-start(f32[384,128]{1,0:T(8,128)} %get-tuple-element.17) | copy-start | bytes 589828
  176.4 10.1 %copy-start = (bf16[16,48,768]{2,1,0:T(8,128)(2,1)S(1)}, bf16[16,48,768]{2,1,0:T(8,128)(2,1)}, u32[]{:S(2)}) copy-start(bf16[16,48,768]{2,1,0:T(8,128)(2,1)} %get-tuple-element.18) | copy-start | bytes 3538948
  186.5 2.9 %copy-start.1 = (f32[2,128,768]{2,1,0:T(8,128)S(1)}, f32[2,128,768]{2,1,0:T(8,128)}, u32[]{:S(2)}) copy-start(f32[2,128,768]{2,1,0:T(8,128)} %get-tuple-element.16) | copy-start | bytes 2359300

commit v3 on v2

--- a/solution.py
+++ b/solution.py
@@ -16,6 +16,7 @@
 CAP = 8
 PARTS = 3
 SMALL = 64
+VMEM_MB = 60
 TANH_A = 0.7978845608
 TANH_B = 0.044715
 
@@ -45,10 +46,10 @@
     x_in, cot_in, routes_in, bucket_in, one_in, two_in, bias_in, router_in, qkv_in, out_in, up_in, down_in,
     sec_out, own_up, own_down, recv_up, recv_down, attn_out, small_out,
     xin, cot, bucket, hot, routes, gain_one, gain_two, bias_w, router, w_qkv, w_out, w_up, w_down,
-    hs, n_one, qkv, probs_s, mixed_s, h_mid_s, n_two, comb, eprobs, x_s, u_s, x_dy, x_du, x_hid, g_s, fin, dqkv,
-    send_a, recv_a, send_c, recv_c, red_a, red_c, red_g, g_up, g_down, chunk, chunk_pair, chunk_in, flat, small, small_pair,
+    hs, n_one, qkv, probs_s, mixed_s, h_mid_s, n_two, comb, eprobs, x_s, u_s, x_dy, x_du, hid_s, g_s, fin, dqkv,
+    send_a, recv_a, send_g, recv_g, send_c, recv_c, red_a, red_c, red_g, g_up, g_down, chunk, chunk_pair, chunk_in, flat, small, small_pair,
     small_in, total, total_small,
-    sem_in, sem_w, sem_ws, sa_send, sa_recv, sc_send, sc_recv, rd_send, rd_recv, rc_send, rc_recv, gr_send, gr_recv, gr_loc,
+    sem_in, sem_w, sem_ws, sa_send, sa_recv, sg_send, sg_recv, sc_send, sc_recv, rd_send, rd_recv, rc_send, rc_recv, gr_send, gr_recv, gr_loc,
     ck_send, ck_recv, pr_send, pr_recv, ag_send, ag_recv, ag_loc, sec_send, sec_recv, sec_loc,
 ):
     ne, nz, seq, width, local, heads, ff, hd = dims
@@ -90,16 +91,31 @@
         (one_in, gain_one), (qkv_in, w_qkv), (bias_in, bias_w), (out_in, w_out), (routes_in, routes), (router_in, router),
         (two_in, gain_two), (up_in, w_up), (down_in, w_down),
     ]
-    for k, (src, dst) in enumerate(weights):
+    def load(k):
+        src, dst = weights[k]
         pltpu.make_async_copy(src.at[p] if k == 4 else src, dst.at[p], sem_w.at[k, p]).start()
-    pl.semaphore_wait(barrier, ne - 1 + nz - 1 + 1)
-    outgoing = []
-    for k, (src, dst) in enumerate(weights):
-        copy = pltpu.make_async_remote_copy(
+
+    def lend(k):
+        src, dst = weights[k]
+        return pltpu.make_async_remote_copy(
             src_ref=src.at[other] if k == 4 else src, dst_ref=dst.at[p], send_sem=sem_ws.at[k], recv_sem=sem_w.at[k, p],
             device_id={"pipe": other}, device_id_type=MESH)
-        copy.start()
-        outgoing.append(copy)
+
+    load(4)
+
+    @pl.when(p == 0)
+    def _():
+        for k in (0, 1, 2, 3, 5, 6):
+            load(k)
+    pl.semaphore_wait(barrier, ne - 1 + nz - 1 + 1)
+    lend(4).start()
+
+    @pl.when(p == 0)
+    def _():
+        for k in (0, 1, 2, 3, 5, 6, 7, 8):
+            lend(k).start()
+        for k in (7, 8):
+            load(k)
 
     def await_weight(k, l):
         dst = weights[k][1]
@@ -121,17 +137,17 @@
         pltpu.make_async_copy(part, part, recv).wait()
 
     def exchange(kind, l):
-        send_all(send_a.at[l, kind], recv_a.at[l, kind], sa_send.at[l, kind], sa_recv.at[l, kind], True)
+        send_all(send_a.at[kind], recv_a.at[l, kind], sa_send.at[l, kind], sa_recv.at[l, kind], True)
 
     def arrived(kind, l):
-        await_all(send_a.at[l, kind], recv_a.at[l, kind], sa_send.at[l, kind], sa_recv.at[l, kind])
+        await_all(send_a.at[kind], recv_a.at[l, kind], sa_send.at[l, kind], sa_recv.at[l, kind])
         return recv_a[l, kind]
 
     def exchange_back(kind, l, c):
-        send_all(send_c.at[l, kind, c], recv_c.at[l, kind, c], sc_send.at[l, kind, c], sc_recv.at[l, kind, c], False)
+        send_all(send_c.at[c], recv_c.at[l, kind, c], sc_send.at[l, kind, c], sc_recv.at[l, kind, c], False)
 
     def arrived_back(kind, l, c):
-        await_all(send_c.at[l, kind, c], recv_c.at[l, kind, c], sc_send.at[l, kind, c], sc_recv.at[l, kind, c])
+        await_all(send_c.at[c], recv_c.at[l, kind, c], sc_send.at[l, kind, c], sc_recv.at[l, kind, c])
         return recv_c[l, kind, c].reshape(slots, part_w)
 
     def reduce_start(buf, send, recv):
@@ -188,6 +204,19 @@
         r = router[l]
         high = r.astype(BF16)
         return high, (r - high.astype(F32)).astype(BF16)
+
+    def place(l):
+        ids = named(l)
+        hot_e = chosen_of(ids)
+        row_at, col_at = lanes_of((seq, seq), 0), lanes_of((seq, seq), 1)
+        earlier = (row_at > col_at).astype(BF16)
+        count = nn(earlier, (hot_e[0] + hot_e[1]).astype(BF16))
+        for kk in range(2):
+            before = count if kk == 0 else count + hot_e[0]
+            c = jnp.sum(before * hot_e[kk], -1, keepdims=True).astype(jnp.int32)
+            e = ids[kk]
+            at = (((e >> 1) - x + ne) & (ne - 1)) * (2 * CAP) + (e & 1) * CAP + c
+            comb[l, kk * seq:(kk + 1) * seq] = (lanes_of((seq, slots), 1) == at).astype(F32).astype(BF16)
 
     def forward(l, _):
         h_in = hs[l]
@@ -219,18 +248,20 @@
         red_a[l, 0, 0] = nn(mixed, w_out[l]).astype(BF16)
         reduce_start(red_a.at[l, 0], rd_send.at[l, 0], rd_recv.at[l, 0])
 
-        await_weight(4, l)
-        ids = named(l)
-        hot_e = chosen_of(ids)
-        row_at, col_at = lanes_of((seq, seq), 0), lanes_of((seq, seq), 1)
-        earlier = (row_at > col_at).astype(BF16)
-        count = nn(earlier, (hot_e[0] + hot_e[1]).astype(BF16))
-        for kk in range(2):
-            before = count if kk == 0 else count + hot_e[0]
-            c = jnp.sum(before * hot_e[kk], -1, keepdims=True).astype(jnp.int32)
-            e = ids[kk]
-            place = (((e >> 1) - x + ne) & (ne - 1)) * (2 * CAP) + (e & 1) * CAP + c
-            comb[l, kk * seq:(kk + 1) * seq] = (lanes_of((seq, slots), 1) == place).astype(F32).astype(BF16)
+        @pl.when(l == 0)
+        def _():
+            @pl.when(p == 1)
+            def _():
+                for k in (0, 1, 2, 3, 5, 6, 7, 8):
+                    lend(k).start()
+                    load(k)
+            for layer in range(2):
+                await_weight(4, layer)
+                place(layer)
+            send_a[1] = tn(comb[1, 0:seq] + comb[1, seq:2 * seq], cot[...]).astype(BF16).reshape(ne, 2 * CAP, width)
+            exchange(1, 1)
+
+        hot_e = chosen_of(named(l))
         both = comb[l, 0:seq] + comb[l, seq:2 * seq]
         await_weight(5, l)
         await_weight(6, l)
@@ -239,7 +270,7 @@
         h_mid_s[l] = h_mid
         n2 = (h_mid * scale_of(h_mid) * gain_two[l]).astype(BF16)
         n_two[l] = n2
-        send_a[l, 0] = tn(both, n2).astype(BF16).reshape(ne, 2 * CAP, width)
+        send_a[0] = tn(both, n2).astype(BF16).reshape(ne, 2 * CAP, width)
         exchange(0, l)
         high, low = router_of(l)
         logits = nt(n2, high) + nt(n2, low)
@@ -249,6 +280,17 @@
         picked = [jnp.sum(ep * hot_e[kk], -1, keepdims=True) for kk in range(2)]
         inv = picked[0] + picked[1]
         gates = [picked[kk] / inv for kk in range(2)]
+
+        @pl.when(l == 1)
+        def _():
+            at = lanes_of((seq, LANES), 1)
+            sent = []
+            for kk in range(2):
+                top = gates[kk].astype(BF16).astype(F32)
+                sent.append(jnp.where(at == 0, top, jnp.where(at == 1, gates[kk] - top, 0.0)).astype(BF16))
+            send_g[...] = tn(comb[l], jnp.concatenate(sent, axis=0)).astype(BF16).reshape(ne, 2 * CAP, LANES)
+            send_all(send_g, recv_g, sg_send, sg_recv, True)
+
         await_weight(7, l)
         await_weight(8, l)
         parts = split(arrived(0, l))
@@ -259,13 +301,20 @@
             u = nn(x_s[l, e], w_up[l, e])
             u_s[l, e] = u
             t = jnp.tanh(TANH_A * (u + TANH_B * u * u * u))
-            x_hid[e] = (0.5 * u * (1.0 + t)).astype(BF16)
+            hid_s[l, e] = (0.5 * u * (1.0 + t)).astype(BF16)
             return 0
         lax.fori_loop(0, local, expert, 0)
         for c in range(parts_c):
             cols = slice(c * part_w, (c + 1) * part_w)
-            send_c[l, 0, c] = join([nn(x_hid[e], w_down[l, e, :, cols]) for e in range(local)])
+            send_c[c] = join([nn(hid_s[l, e], w_down[l, e, :, cols]) for e in range(local)])
             exchange_back(0, l, c)
+
+        def slopes(e, _):
+            u = u_s[l, e]
+            t = jnp.tanh(TANH_A * (u + TANH_B * u * u * u))
+            u_s[l, e] = 0.5 * (1.0 + t) + (0.5 * TANH_A) * u * (1.0 - t * t) * (1.0 + (3.0 * TANH_B) * u * u)
+            return 0
+        lax.fori_loop(0, local, slopes, 0)
         out = summed_back(0, l, lambda back: gates[0] * nn(comb[l, 0:seq], back) + gates[1] * nn(comb[l, seq:2 * seq], back))
         out = h_mid + out()
         hs[l + 1] = jnp.where(l == 0, out.astype(BF16).astype(F32), out)
@@ -341,6 +390,8 @@
         pltpu.make_async_remote_copy(
             src_ref=src, dst_ref=dst, send_sem=send, recv_sem=recv, device_id={"pipe": other}, device_id_type=MESH).start()
 
+    part = send_a.at[1, pl.ds(1, ne - 1)]
+    pltpu.make_async_copy(part, part, sa_send.at[1, 1]).wait()
     deliver(hs.at[2], 1)
     g_s[...] = cot[...].astype(F32)
 
@@ -352,16 +403,48 @@
         picked = [jnp.sum(ep * hot_e[kk], -1, keepdims=True) for kk in range(2)]
         inv = picked[0] + picked[1]
         gates = [picked[kk] / inv for kk in range(2)]
-        dy = jnp.concatenate([(gates[kk] * g).astype(BF16) for kk in range(2)], axis=0)
-        send_a[l, 1] = tn(comb[l], dy).astype(BF16).reshape(ne, 2 * CAP, width)
-        exchange(1, l)
+        at = lanes_of((seq, LANES), 1)
+
+        @pl.when(l == 0)
+        def _():
+            dy = jnp.concatenate([(gates[kk] * g).astype(BF16) for kk in range(2)], axis=0)
+            send_a[1] = tn(comb[l], dy).astype(BF16).reshape(ne, 2 * CAP, width)
+            exchange(1, l)
+
+            @pl.when(p == 1)
+            def _():
+                merge_attn()
+                merge_small()
+            parts = split(arrived(1, l))
+            for e in range(local):
+                x_dy[e] = parts[e]
+
+        @pl.when(l == 1)
+        def _():
+            await_all(send_g, recv_g, sg_send, sg_recv)
+            weigh = jnp.sum(recv_g[...].astype(F32), -1, keepdims=True)
+            part = recv_a.at[l, 1, pl.ds(1, ne - 1)]
+            pltpu.make_async_copy(part, part, sa_recv.at[l, 1]).wait()
+            wide = recv_a[l, 1].astype(F32) * weigh
+            for e in range(local):
+                x_dy[e] = wide[:, e * CAP:(e + 1) * CAP].reshape(ne * CAP, width).astype(BF16)
+
+        def expert(e, _):
+            dy_e = x_dy[e]
+            dh = nt(dy_e, w_down[l, e])
+            x_du[e] = (dh * u_s[l, e]).astype(BF16)
+            return 0
+        lax.fori_loop(0, local, expert, 0)
+        for c in range(parts_c):
+            cols = slice(c * part_w, (c + 1) * part_w)
+            send_c[c] = join([nt(x_du[e], w_up[l, e, cols]) for e in range(local)])
+            exchange_back(1, l, c)
 
         @pl.when((p == 1) & (l == 0))
         def _():
-            merge_attn()
-            merge_small()
-
-        at = lanes_of((seq, LANES), 1)
+            spread_attn()
+            spread_small()
+
         gg = jnp.zeros((seq, LANES), F32)
         for kk in range(2):
             part = None
@@ -373,34 +456,10 @@
             gg = gg + jnp.where(at == kk, high, 0.0) + jnp.where(at == 2 + kk, part - high, 0.0)
         red_g[l, 0] = gg.astype(BF16)
         reduce_start(red_g.at[l], rd_send.at[l, 2], rd_recv.at[l, 2])
-        parts = split(arrived(1, l))
-        for e in range(local):
-            x_dy[e] = parts[e]
-
-        def expert(e, _):
-            dy_e = x_dy[e]
-            dh = nt(dy_e, w_down[l, e])
-            u = u_s[l, e]
-            t = jnp.tanh(TANH_A * (u + TANH_B * u * u * u))
-            slope = 0.5 * (1.0 + t) + (0.5 * TANH_A) * u * (1.0 - t * t) * (1.0 + (3.0 * TANH_B) * u * u)
-            du = (dh * slope).astype(BF16)
-            x_du[e] = du
-            x_hid[e] = (0.5 * u * (1.0 + t)).astype(BF16)
-            return 0
-        lax.fori_loop(0, local, expert, 0)
-        for c in range(parts_c):
-            cols = slice(c * part_w, (c + 1) * part_w)
-            send_c[l, 1, c] = join([nt(x_du[e], w_up[l, e, cols]) for e in range(local)])
-            exchange_back(1, l, c)
-
-        @pl.when((p == 1) & (l == 0))
-        def _():
-            spread_attn()
-            spread_small()
 
         def expert_grads(e, _):
             g_up[l, e] = tn(x_s[l, e], x_du[e]).astype(BF16)
-            g_down[l, e] = tn(x_hid[e], x_dy[e]).astype(BF16)
+            g_down[l, e] = tn(hid_s[l, e], x_dy[e]).astype(BF16)
             return 0
         lax.fori_loop(0, local, expert_grads, 0)
 
@@ -433,7 +492,6 @@
         dg = dn2 * gain_two[l]
         dmid = g + scale * dg - h_mid * (scale * scale * scale) * jnp.mean(h_mid * dg, -1, keepdims=True)
         da = dmid.astype(BF16)
-        chunk[l, 3 * per:4 * per] = tn(mixed_s[l], da).astype(BF16).reshape(per, rows, width)
         dmixed = nt(da, w_out[l]).astype(BF16)
         q, k, v = qkv[l, 0], qkv[l, 1], qkv[l, 2]
         dq = jnp.zeros((seq, hw), F32)
@@ -465,6 +523,7 @@
         red_a[l, 1, 0] = dn1.astype(BF16)
         reduce_start(red_a.at[l, 1], rd_send.at[l, 1], rd_recv.at[l, 1])
         n1 = n_one[l]
+        chunk[l, 3 * per:4 * per] = tn(mixed_s[l], da).astype(BF16).reshape(per, rows, width)
         for c in range(3):
             chunk[l, c * per:(c + 1) * per] = tn(dqkv[c], n1).astype(BF16).reshape(per, rows, width)
 
@@ -506,8 +565,8 @@
         spread_attn()
         spread_small()
 
-    for copy in outgoing:
-        copy.wait_send()
+    for k in range(len(weights)):
+        lend(k).wait_send()
     for k, ref in enumerate((g_up, g_down)):
         for sem in (gr_loc, gr_send, gr_recv):
             pltpu.make_async_copy(ref.at[0], ref.at[0], sem.at[k]).wait()
@@ -542,6 +601,7 @@
     slots = ne * local * CAP
 
     any_space = pl.BlockSpec(memory_space=pl.ANY)
+    hbm = pl.BlockSpec(memory_space=pltpu.HBM)
     vm = pltpu.VMEM
     dma = pltpu.SemaphoreType.DMA
     sds = jax.ShapeDtypeStruct
@@ -555,7 +615,7 @@
             sds((micro, seq, width), F32), sds(half, BF16), sds(half, BF16), sds(half, BF16), sds(half, BF16),
             sds((ne, rows, width), BF16), sds((flat, LANES), F32),
         ],
-        in_specs=[any_space] * 12,
+        in_specs=[hbm] * 12,
         out_specs=[any_space] * 7,
         scratch_shapes=[
             vm((seq, width), BF16), vm((seq, width), BF16), vm((1, seq), jnp.int32), vm((seq, buckets), F32),
@@ -566,19 +626,20 @@
             vm((2, heads, seq, seq), F32), vm((2, seq, hw), BF16), vm((2, seq, width), F32), vm((2, seq, width), BF16),
             vm((2, 2 * seq, slots), BF16), vm((2, seq, experts), F32), vm((2, local, ne * CAP, width), BF16),
             vm((2, local, ne * CAP, ff), F32),
-            vm((local, ne * CAP, width), BF16), vm((local, ne * CAP, ff), BF16), vm((local, ne * CAP, ff), BF16),
+            vm((local, ne * CAP, width), BF16), vm((local, ne * CAP, ff), BF16), vm((2, local, ne * CAP, ff), BF16),
             vm((seq, width), F32), vm((seq, width), F32), vm((3, seq, hw), BF16),
-            vm((2, 2, ne, 2 * CAP, width), BF16), vm((2, 2, ne, 2 * CAP, width), BF16), vm(parts_in, BF16), vm(parts_in, BF16),
+            vm((2, ne, 2 * CAP, width), BF16), vm((2, 2, ne, 2 * CAP, width), BF16), vm((ne, 2 * CAP, LANES), BF16),
+            vm((ne, 2 * CAP, LANES), BF16), vm(parts_in[2:], BF16), vm(parts_in, BF16),
             vm((2, 2, nz, seq, width), BF16), vm((2, 2, PARTS, nz, seq, part_w), BF16), vm((2, nz, seq, LANES), BF16),
             vm((2, *half), BF16), vm((2, *half), BF16), vm((2, ne, rows, width), BF16), vm((ne, rows, width), BF16),
             vm((ne, rows, width), BF16), vm((SMALL, width), F32), vm((2, flat, LANES), F32), vm((flat, LANES), F32),
             vm((ne, flat // ne, LANES), F32), vm((rows, width), BF16), vm((flat // ne, LANES), F32),
-            dma((3,)), dma((9, 2)), dma((9,)), dma((2, 2)), dma((2, 2)), dma((2, 2, PARTS)), dma((2, 2, PARTS)),
+            dma((3,)), dma((9, 2)), dma((9,)), dma((2, 2)), dma((2, 2)), dma, dma, dma((2, 2, PARTS)), dma((2, 2, PARTS)),
             dma((2, 3)), dma((2, 3)), dma((2, 2, PARTS)), dma((2, 2, PARTS)), dma((2,)), dma((2,)), dma((2,)),
             dma((2,)), dma((2,)), dma((2,)), dma((2,)), dma((2,)), dma((2,)), dma((2,)), dma, dma, dma,
         ],
         compiler_params=pltpu.CompilerParams(
-            collective_id=0, has_side_effects=True, vmem_limit_bytes=60 * 1024 * 1024),
+            collective_id=0, has_side_effects=True, vmem_limit_bytes=VMEM_MB * 1024 * 1024),
         cost_estimate=pl.CostEstimate(flops=20_000_000_000, bytes_accessed=40_000_000, transcendentals=2_000_000),
     )(
         block_input, cotangent, routes[0].transpose(0, 2, 1), offset_bucket[None], norm1_gain, norm2_gain,

time: 190 us -> 185 us (0.974)
  Pallas kernels: 176 us -> 170 us
    pallas_call x1, Pallas kernels: 176 us -> 170 us  [body(): pl.pallas_call(functools.partial(kernel, (ne, nz, seq, width, local, head...]
where the time goes in v3:
time: 185 us
  Pallas kernels  170 us (92%)
  other arithmetic  8.65 us (5%)
  local copies, waits for them, and re-layouts  5.12 us (3%)
    pallas_call x1, Pallas kernels, body(): pl.pallas_call(functools.partial(kernel, (ne, nz, seq, width, local, head...  170 us
    broadcast_in_dim x1, other arithmetic, body(): grad_down[None]  8.65 us

profile of v3, /device:TPU:0, one launch (start us, length us, event | category | flops | bytes accessed | tf_op | source)
XLA Modules:
  0.0 184.6 jit_solution(7342282866304401917)
XLA Ops:
  0.6 170.2 %shard_map.187 = (f32[2,128,768]{2,1,0:T(8,128)}, bf16[2,768,768]{2,1,0:T(8,128)(2,1)}, bf16[2,768,768]{2,1,0:T(8,128)(2,1)}, bf16[2,768,768]{2,1,0:T(8,128)(2,1...) custom-call(bf16[2,128,768]{2,1,0:T(8,128)(2,1)} %x_in.1, ...), custom_call_target="tpu_custom_call" | custom-call | flops 20000000000 | bytes 40000000 | tf_op jit(solution)/shard_map/pallas_call | solution.py:612
  170.8 0.0 copy-start.2
  170.8 0.0 copy-start
  170.8 8.7 %add_bitcast_fusion = (f32[1,2,768,768]{3,2,1,0:T(8,128)}, f32[1,2,768,768]{3,2,1,0:T(8,128)}) fusion(bf16[2,768,768]{2,1,0:T(8,128)(2,1)} %get-tuple-element.22, bf16[2,768,768]{2,1,0:T(8,128)(2,1)} %get-tuple-element.21, bf16[2,768,768]{2,1,0:T(8,128)(2,1)} %get-tuple-element.20, bf16[2,768,768]{2,1,0:T(8,128)(2,1)} %get-tuple-element.19), kind=kLoop, calls=%fused_computation | loop fusion | flops 7077888 | bytes 18874368 | tf_op jit(solution)/shard_map/broadcast_in_dim | solution.py:656
  179.5 0.0 copy-done.2
  179.5 0.1 copy.40
  179.6 0.6 copy_bitcast_fusion.2
  180.2 0.7 copy.39
  180.9 0.0 copy-done
  180.9 0.0 copy-start.1
  180.9 1.4 slice.42
  182.3 0.9 slice.43
  183.2 0.6 copy.27
  183.8 0.0 copy-done.1
  183.8 0.9 copy.42
  (4 shorter events, 0.1 us)
Async XLA Ops:
  170.8 8.7 %copy-start.2 = (f32[384,128]{1,0:T(8,128)S(1)}, f32[384,128]{1,0:T(8,128)}, u32[]{:S(2)}) copy-start(f32[384,128]{1,0:T(8,128)} %get-tuple-element.17) | copy-start | bytes 589828
  170.8 10.1 %copy-start = (bf16[16,48,768]{2,1,0:T(8,128)(2,1)S(1)}, bf16[16,48,768]{2,1,0:T(8,128)(2,1)}, u32[]{:S(2)}) copy-start(bf16[16,48,768]{2,1,0:T(8,128)(2,1)} %get-tuple-element.18) | copy-start | bytes 3538948
  180.9 2.9 %copy-start.1 = (f32[2,128,768]{2,1,0:T(8,128)S(1)}, f32[2,128,768]{2,1,0:T(8,128)}, u32[]{:S(2)}) copy-start(f32[2,128,768]{2,1,0:T(8,128)} %get-tuple-element.16) | copy-start | bytes 2359300

commit v4 on v3

--- a/solution.py
+++ b/solution.py
@@ -45,11 +45,11 @@
     dims,
     x_in, cot_in, routes_in, bucket_in, one_in, two_in, bias_in, router_in, qkv_in, out_in, up_in, down_in,
     sec_out, own_up, own_down, recv_up, recv_down, attn_out, small_out,
-    xin, cot, bucket, hot, routes, gain_one, gain_two, bias_w, router, w_qkv, w_out, w_up, w_down,
+    xin, cot, bucket, hot, routes, gain_one, gain_two, bias_w, router, w_qkv, w_full, w_up, w_down,
     hs, n_one, qkv, probs_s, mixed_s, h_mid_s, n_two, comb, eprobs, x_s, u_s, x_dy, x_du, hid_s, g_s, fin, dqkv,
-    send_a, recv_a, send_g, recv_g, send_c, recv_c, red_a, red_c, red_g, g_up, g_down, chunk, chunk_pair, chunk_in, flat, small, small_pair,
+    send_a, recv_a, send_g, recv_g, send_c, recv_c, mix, red_a, red_c, red_g, g_up, g_down, chunk, chunk_pair, chunk_in, flat, small, small_pair,
     small_in, total, total_small,
-    sem_in, sem_w, sem_ws, sa_send, sa_recv, sg_send, sg_recv, sc_send, sc_recv, rd_send, rd_recv, rc_send, rc_recv, gr_send, gr_recv, gr_loc,
+    sem_in, sem_w, sem_ws, wo_send, wo_recv, mx_send, mx_recv, sa_send, sa_recv, sg_send, sg_recv, sc_send, sc_recv, rd_send, rd_recv, rc_send, rc_recv, gr_send, gr_recv, gr_loc,
     ck_send, ck_recv, pr_send, pr_recv, ag_send, ag_recv, ag_loc, sec_send, sec_recv, sec_loc,
 ):
     ne, nz, seq, width, local, heads, ff, hd = dims
@@ -88,7 +88,7 @@
     for copy in ins:
         copy.start()
     weights = [
-        (one_in, gain_one), (qkv_in, w_qkv), (bias_in, bias_w), (out_in, w_out), (routes_in, routes), (router_in, router),
+        (one_in, gain_one), (qkv_in, w_qkv), (bias_in, bias_w), (w_full, w_full), (routes_in, routes), (router_in, router),
         (two_in, gain_two), (up_in, w_up), (down_in, w_down),
     ]
     def load(k):
@@ -98,21 +98,39 @@
     def lend(k):
         src, dst = weights[k]
         return pltpu.make_async_remote_copy(
-            src_ref=src.at[other] if k == 4 else src, dst_ref=dst.at[p], send_sem=sem_ws.at[k], recv_sem=sem_w.at[k, p],
+            src_ref=src.at[other] if k == 4 else src.at[p] if k == 3 else src, dst_ref=dst.at[p], send_sem=sem_ws.at[k], recv_sem=sem_w.at[k, p],
             device_id={"pipe": other}, device_id_type=MESH)
+
+    def gather_start():
+        pltpu.make_async_copy(out_in, w_full.at[p, z], sem_in.at[3]).start()
+
+        def one(r, _):
+            pltpu.make_async_remote_copy(
+                src_ref=out_in, dst_ref=w_full.at[p, z], send_sem=wo_send, recv_sem=wo_recv,
+                device_id={"tensor": lax.rem(z + r, nz)}, device_id_type=MESH).start()
+            return 0
+        lax.fori_loop(1, nz, one, 0)
+
+    def gather_end():
+        pltpu.make_async_copy(out_in, w_full.at[p, z], sem_in.at[3]).wait()
+        part = w_full.at[p, pl.ds(1, nz - 1)]
+        pltpu.make_async_copy(part, part, wo_send).wait()
+        pltpu.make_async_copy(part, part, wo_recv).wait()
+        lend(3).start()
 
     load(4)
 
     @pl.when(p == 0)
     def _():
-        for k in (0, 1, 2, 3, 5, 6):
+        for k in (0, 1, 2, 5, 6):
             load(k)
     pl.semaphore_wait(barrier, ne - 1 + nz - 1 + 1)
     lend(4).start()
 
     @pl.when(p == 0)
     def _():
-        for k in (0, 1, 2, 3, 5, 6, 7, 8):
+        gather_start()
+        for k in (0, 1, 2, 5, 6, 7, 8):
             lend(k).start()
         for k in (7, 8):
             load(k)
@@ -244,15 +262,15 @@
             mixed = mixed + nn(prob.astype(BF16), v * mask)
         mixed = mixed.astype(BF16)
         mixed_s[l] = mixed
-        await_weight(3, l)
-        red_a[l, 0, 0] = nn(mixed, w_out[l]).astype(BF16)
-        reduce_start(red_a.at[l, 0], rd_send.at[l, 0], rd_recv.at[l, 0])
+        mix[l, 0] = mixed
+        reduce_start(mix.at[l], mx_send.at[l], mx_recv.at[l])
 
         @pl.when(l == 0)
         def _():
             @pl.when(p == 1)
             def _():
-                for k in (0, 1, 2, 3, 5, 6, 7, 8):
+                gather_start()
+                for k in (0, 1, 2, 5, 6, 7, 8):
                     lend(k).start()
                     load(k)
             for layer in range(2):
@@ -266,7 +284,22 @@
         await_weight(5, l)
         await_weight(6, l)
 
-        h_mid = h_in + reduce_end(red_a.at[l, 0], rd_send.at[l, 0], rd_recv.at[l, 0])
+        @pl.when((p == 0) & (l == 0))
+        def _():
+            gather_end()
+
+        @pl.when(l != p)
+        def _():
+            await_weight(3, l)
+
+        part = mix.at[l, pl.ds(1, nz - 1)]
+        pltpu.make_async_copy(part, part, mx_send.at[l]).wait()
+        pltpu.make_async_copy(part, part, mx_recv.at[l]).wait()
+        attn = None
+        for a in range(nz):
+            term = nn(mix[l, lax.rem(z + nz - a, nz)], w_full[l, a])
+            attn = term if attn is None else attn + term
+        h_mid = h_in + attn
         h_mid_s[l] = h_mid
         n2 = (h_mid * scale_of(h_mid) * gain_two[l]).astype(BF16)
         n_two[l] = n2
@@ -309,6 +342,10 @@
             send_c[c] = join([nn(hid_s[l, e], w_down[l, e, :, cols]) for e in range(local)])
             exchange_back(0, l, c)
 
+        @pl.when((p == 1) & (l == 0))
+        def _():
+            gather_end()
+
         def slopes(e, _):
             u = u_s[l, e]
             t = jnp.tanh(TANH_A * (u + TANH_B * u * u * u))
@@ -340,27 +377,34 @@
                 src_ref=src, dst_ref=sec_out.at[p], send_sem=sec_send, recv_sem=sec_recv,
                 device_id={"pipe": other}, device_id_type=MESH).start()
 
-    def merge(k, src, pair, mine, within, dst, send, recv):
-        pltpu.make_async_copy(pair, pair, pr_recv.at[k]).wait()
-        mine[...] = (src[p].astype(F32) + pair[...].astype(F32)).astype(mine.dtype)
+    def piece(ref, j):
+        return ref.at[pl.ds(pl.multiple_of(j * flat_rows, 8), flat_rows)]
+
+    def merge_attn():
+        pltpu.make_async_copy(chunk_pair, chunk_pair, pr_recv.at[0]).wait()
+        for c in range(parts_c):
+            chunk_pair[c] = (chunk[p, c].astype(F32) + chunk_pair[c].astype(F32)).astype(BF16)
+
+            def scatter(r, _, c=c):
+                to = lax.rem(x + r, ne)
+                pltpu.make_async_remote_copy(
+                    src_ref=chunk_pair.at[c, to], dst_ref=chunk_in.at[c, r], send_sem=ck_send.at[c], recv_sem=ck_recv.at[c],
+                    device_id={"expert": to}, device_id_type=MESH).start()
+                return 0
+            lax.fori_loop(1, ne, scatter, 0)
+            chunk_in[c, 0] = chunk_pair[c, x]
+
+    def merge_small():
+        pltpu.make_async_copy(small_pair, small_pair, pr_recv.at[1]).wait()
+        small_pair[...] = small[p] + small_pair[...]
 
         def scatter(r, _):
             to = lax.rem(x + r, ne)
             pltpu.make_async_remote_copy(
-                src_ref=within(mine, to), dst_ref=dst.at[r], send_sem=send, recv_sem=recv,
+                src_ref=piece(small_pair, to), dst_ref=small_in.at[r], send_sem=ck_send.at[parts_c], recv_sem=ck_recv.at[parts_c],
                 device_id={"expert": to}, device_id_type=MESH).start()
             return 0
         lax.fori_loop(1, ne, scatter, 0)
-
-    def merge_attn():
-        merge(0, chunk, chunk_pair, chunk_pair, lambda ref, j: ref.at[j], chunk_in, ck_send.at[0], ck_recv.at[0])
-        chunk_in[0] = chunk_pair[x]
-
-    def piece(ref, j):
-        return ref.at[pl.ds(pl.multiple_of(j * flat_rows, 8), flat_rows)]
-
-    def merge_small():
-        merge(1, small, small_pair, small_pair, piece, small_in, ck_send.at[1], ck_recv.at[1])
         small_in[0] = small_pair[pl.ds(pl.multiple_of(x * flat_rows, 8), flat_rows)]
 
     def spread(k, arrived_at, whole, dst):
@@ -381,10 +425,11 @@
         lax.fori_loop(1, ne, one, 0)
 
     def spread_attn():
-        spread(0, chunk_in, total, attn_out.at[x])
+        for c in range(parts_c):
+            spread(c, chunk_in.at[c], total.at[c], attn_out.at[x, :, pl.ds(c * part_w, part_w)])
 
     def spread_small():
-        spread(1, small_in, total_small, piece(small_out, x))
+        spread(parts_c, small_in, total_small, piece(small_out, x))
 
     def to_partner(src, dst, send, recv):
         pltpu.make_async_remote_copy(
@@ -394,6 +439,11 @@
     pltpu.make_async_copy(part, part, sa_send.at[1, 1]).wait()
     deliver(hs.at[2], 1)
     g_s[...] = cot[...].astype(F32)
+
+    def keep_grad(l, k, value):
+        value = value.astype(BF16)
+        for c in range(parts_c):
+            chunk[l, c, k * per:(k + 1) * per] = value[:, c * part_w:(c + 1) * part_w].reshape(per, rows, part_w)
 
     def backward(i, _):
         l = 1 - i
@@ -455,7 +505,7 @@
             high = part.astype(BF16).astype(F32)
             gg = gg + jnp.where(at == kk, high, 0.0) + jnp.where(at == 2 + kk, part - high, 0.0)
         red_g[l, 0] = gg.astype(BF16)
-        reduce_start(red_g.at[l], rd_send.at[l, 2], rd_recv.at[l, 2])
+        reduce_start(red_g.at[l], rd_send.at[l, 1], rd_recv.at[l, 1])
 
         def expert_grads(e, _):
             g_up[l, e] = tn(x_s[l, e], x_du[e]).astype(BF16)
@@ -478,7 +528,7 @@
 
         h_mid = h_mid_s[l]
         scale = scale_of(h_mid)
-        tail = reduce_end(red_g.at[l], rd_send.at[l, 2], rd_recv.at[l, 2])
+        tail = reduce_end(red_g.at[l], rd_send.at[l, 1], rd_recv.at[l, 1])
         dn2 = dn2()
         gg = [jnp.sum(jnp.where((at == kk) | (at == 2 + kk), tail, 0.0), -1, keepdims=True) for kk in range(2)]
         centre = gg[0] * gates[0] + gg[1] * gates[1]
@@ -492,7 +542,7 @@
         dg = dn2 * gain_two[l]
         dmid = g + scale * dg - h_mid * (scale * scale * scale) * jnp.mean(h_mid * dg, -1, keepdims=True)
         da = dmid.astype(BF16)
-        dmixed = nt(da, w_out[l]).astype(BF16)
+        dmixed = nt(da, w_full[l, z]).astype(BF16)
         q, k, v = qkv[l, 0], qkv[l, 1], qkv[l, 2]
         dq = jnp.zeros((seq, hw), F32)
         dk = jnp.zeros((seq, hw), F32)
@@ -520,12 +570,12 @@
         dqkv[1] = (dk * (hd ** -0.5)).astype(BF16)
         dqkv[2] = dv.astype(BF16)
         dn1 = nn(dqkv[0], w_qkv[l, 0]) + nn(dqkv[1], w_qkv[l, 1]) + nn(dqkv[2], w_qkv[l, 2])
-        red_a[l, 1, 0] = dn1.astype(BF16)
-        reduce_start(red_a.at[l, 1], rd_send.at[l, 1], rd_recv.at[l, 1])
+        red_a[l, 0] = dn1.astype(BF16)
+        reduce_start(red_a.at[l], rd_send.at[l, 0], rd_recv.at[l, 0])
         n1 = n_one[l]
-        chunk[l, 3 * per:4 * per] = tn(mixed_s[l], da).astype(BF16).reshape(per, rows, width)
+        keep_grad(l, 3, tn(mixed_s[l], da))
         for c in range(3):
-            chunk[l, c * per:(c + 1) * per] = tn(dqkv[c], n1).astype(BF16).reshape(per, rows, width)
+            keep_grad(l, c, tn(dqkv[c], n1))
 
         @pl.when(p != l)
         def _():
@@ -541,7 +591,7 @@
         flat[ne * local + 8:ne * local + 16, 0:hot.shape[1]] = nn(bias_high, hot_b) + nn(bias_low, hot_b)
         h_in = hs[l]
         scale_one = scale_of(h_in)
-        dn1 = reduce_end(red_a.at[l, 1], rd_send.at[l, 1], rd_recv.at[l, 1])
+        dn1 = reduce_end(red_a.at[l], rd_send.at[l, 0], rd_recv.at[l, 0])
         flat[ne * local:ne * local + 1] = jnp.sum(dn1 * h_in * scale_one, 0, keepdims=True)
         for b in range(fold):
             small[l, b * SMALL:(b + 1) * SMALL] = flat[:, b * LANES:(b + 1) * LANES]
@@ -572,8 +622,10 @@
             pltpu.make_async_copy(ref.at[0], ref.at[0], sem.at[k]).wait()
     for sem in (sec_loc, sec_send, sec_recv):
         pltpu.make_async_copy(fin, fin, sem).wait()
-    for k, (pair, whole, arrived_at) in enumerate(((chunk_pair, total, chunk_in), (small_pair, total_small, small_in))):
+    for k, pair in enumerate((chunk_pair, small_pair)):
         pltpu.make_async_copy(pair, pair, pr_send.at[k]).wait()
+    for k in range(parts_c + 1):
+        whole, arrived_at = (total.at[k], chunk_in.at[k]) if k < parts_c else (total_small, small_in)
         pltpu.make_async_copy(whole, whole, ag_loc.at[k]).wait()
         part = arrived_at.at[pl.ds(1, ne - 1)]
         pltpu.make_async_copy(part, part, ag_send.at[k]).wait()
@@ -609,6 +661,7 @@
     flat = width // LANES * SMALL
     parts_in = (2, 2, PARTS, ne, 2 * CAP, part_w)
     half = (local, width, ff)
+    cut = (PARTS, ne, rows, part_w)
     sec, own_up, own_down, recv_up, recv_down, attn, small = pl.pallas_call(
         functools.partial(kernel, (ne, nz, seq, width, local, heads, ff, hd)),
         out_shape=[
@@ -621,7 +674,7 @@
             vm((seq, width), BF16), vm((seq, width), BF16), vm((1, seq), jnp.int32), vm((seq, buckets), F32),
             vm((2, 2, seq), jnp.int32), vm((2, 1, width), F32), vm((2, 1, width), F32), vm((2, heads, 1, buckets), F32),
             vm((2, experts, width), F32), vm((2, 3, hw, width), BF16),
-            vm((2, hw, width), BF16), vm((2, local, width, ff), BF16), vm((2, local, ff, width), BF16),
+            vm((2, nz, hw, width), BF16), vm((2, local, width, ff), BF16), vm((2, local, ff, width), BF16),
             vm((3, seq, width), F32), vm((2, seq, width), BF16), vm((2, 3, seq, hw), BF16),
             vm((2, heads, seq, seq), F32), vm((2, seq, hw), BF16), vm((2, seq, width), F32), vm((2, seq, width), BF16),
             vm((2, 2 * seq, slots), BF16), vm((2, seq, experts), F32), vm((2, local, ne * CAP, width), BF16),
@@ -630,13 +683,14 @@
             vm((seq, width), F32), vm((seq, width), F32), vm((3, seq, hw), BF16),
             vm((2, ne, 2 * CAP, width), BF16), vm((2, 2, ne, 2 * CAP, width), BF16), vm((ne, 2 * CAP, LANES), BF16),
             vm((ne, 2 * CAP, LANES), BF16), vm(parts_in[2:], BF16), vm(parts_in, BF16),
-            vm((2, 2, nz, seq, width), BF16), vm((2, 2, PARTS, nz, seq, part_w), BF16), vm((2, nz, seq, LANES), BF16),
-            vm((2, *half), BF16), vm((2, *half), BF16), vm((2, ne, rows, width), BF16), vm((ne, rows, width), BF16),
-            vm((ne, rows, width), BF16), vm((SMALL, width), F32), vm((2, flat, LANES), F32), vm((flat, LANES), F32),
-            vm((ne, flat // ne, LANES), F32), vm((rows, width), BF16), vm((flat // ne, LANES), F32),
-            dma((3,)), dma((9, 2)), dma((9,)), dma((2, 2)), dma((2, 2)), dma, dma, dma((2, 2, PARTS)), dma((2, 2, PARTS)),
-            dma((2, 3)), dma((2, 3)), dma((2, 2, PARTS)), dma((2, 2, PARTS)), dma((2,)), dma((2,)), dma((2,)),
-            dma((2,)), dma((2,)), dma((2,)), dma((2,)), dma((2,)), dma((2,)), dma((2,)), dma, dma, dma,
+            vm((2, nz, seq, hw), BF16), vm((2, nz, seq, width), BF16), vm((2, 2, PARTS, nz, seq, part_w), BF16), vm((2, nz, seq, LANES), BF16),
+            vm((2, *half), BF16), vm((2, *half), BF16), vm((2, *cut), BF16), vm(cut, BF16),
+            vm(cut, BF16), vm((SMALL, width), F32), vm((2, flat, LANES), F32), vm((flat, LANES), F32),
+            vm((ne, flat // ne, LANES), F32), vm((PARTS, rows, part_w), BF16), vm((flat // ne, LANES), F32),
+            dma((4,)), dma((9, 2)), dma((9,)), dma, dma, dma((2,)), dma((2,)), dma((2, 2)), dma((2, 2)), dma, dma, dma((2, 2, PARTS)), dma((2, 2, PARTS)),
+            dma((2, 2)), dma((2, 2)), dma((2, 2, PARTS)), dma((2, 2, PARTS)), dma((2,)), dma((2,)), dma((2,)),
+            dma((PARTS + 1,)), dma((PARTS + 1,)), dma((2,)), dma((2,)), dma((PARTS + 1,)), dma((PARTS + 1,)), dma((PARTS + 1,)),
+            dma, dma, dma,
         ],
         compiler_params=pltpu.CompilerParams(
             collective_id=0, has_side_effects=True, vmem_limit_bytes=VMEM_MB * 1024 * 1024),

time: 185 us -> 177 us (0.957)
  Pallas kernels: 170 us -> 161 us
    pallas_call x1, Pallas kernels: 170 us -> 161 us  [body(): pl.pallas_call(functools.partial(kernel, (ne, nz, seq, width, local, head...]
where the time goes in v4:
time: 177 us; the launch traced here: 176 us
  Pallas kernels  161 us (91%)
  other arithmetic  8.65 us (5%)
  local copies, waits for them, and re-layouts  5.12 us (3%)
    pallas_call x1, Pallas kernels, body(): pl.pallas_call(functools.partial(kernel, (ne, nz, seq, width, local, head...  161 us
    broadcast_in_dim x1, other arithmetic, body(): grad_down[None]  8.65 us

profile of v4, /device:TPU:0, one launch (start us, length us, event | category | flops | bytes accessed | tf_op | source)
XLA Modules:
  0.0 175.7 jit_solution(9823979521409158079)
XLA Ops:
  0.6 161.2 %shard_map.187 = (f32[2,128,768]{2,1,0:T(8,128)}, bf16[2,768,768]{2,1,0:T(8,128)(2,1)}, bf16[2,768,768]{2,1,0:T(8,128)(2,1)}, bf16[2,768,768]{2,1,0:T(8,128)(2,1...) custom-call(bf16[2,128,768]{2,1,0:T(8,128)(2,1)} %x_in.1, ...), custom_call_target="tpu_custom_call" | custom-call | flops 20000000000 | bytes 40000000 | tf_op jit(solution)/shard_map/pallas_call | solution.py:665
  161.9 0.0 copy-start.2
  161.9 0.0 copy-start
  161.9 8.7 %add_bitcast_fusion = (f32[1,2,768,768]{3,2,1,0:T(8,128)}, f32[1,2,768,768]{3,2,1,0:T(8,128)}) fusion(bf16[2,768,768]{2,1,0:T(8,128)(2,1)} %get-tuple-element.22, bf16[2,768,768]{2,1,0:T(8,128)(2,1)} %get-tuple-element.21, bf16[2,768,768]{2,1,0:T(8,128)(2,1)} %get-tuple-element.20, bf16[2,768,768]{2,1,0:T(8,128)(2,1)} %get-tuple-element.19), kind=kLoop, calls=%fused_computation | loop fusion | flops 7077888 | bytes 18874368 | tf_op jit(solution)/shard_map/broadcast_in_dim | solution.py:710
  170.6 0.0 copy-done.2
  170.6 0.1 copy.40
  170.7 0.6 copy_bitcast_fusion.2
  171.3 0.7 copy.39
  172.0 0.0 copy-done
  172.0 0.0 copy-start.1
  172.0 1.4 slice.42
  173.3 0.9 slice.43
  174.2 0.6 copy.27
  174.8 0.0 copy-done.1
  174.8 0.9 copy.42
  (4 shorter events, 0.1 us)
Async XLA Ops:
  161.9 8.7 %copy-start.2 = (f32[384,128]{1,0:T(8,128)S(1)}, f32[384,128]{1,0:T(8,128)}, u32[]{:S(2)}) copy-start(f32[384,128]{1,0:T(8,128)} %get-tuple-element.17) | copy-start | bytes 589828
  161.9 10.1 %copy-start = (bf16[16,48,768]{2,1,0:T(8,128)(2,1)S(1)}, bf16[16,48,768]{2,1,0:T(8,128)(2,1)}, u32[]{:S(2)}) copy-start(bf16[16,48,768]{2,1,0:T(8,128)(2,1)} %get-tuple-element.18) | copy-start | bytes 3538948
  172.0 2.9 %copy-start.1 = (f32[2,128,768]{2,1,0:T(8,128)S(1)}, f32[2,128,768]{2,1,0:T(8,128)}, u32[]{:S(2)}) copy-start(f32[2,128,768]{2,1,0:T(8,128)} %get-tuple-element.16) | copy-start | bytes 2359300

commit v5 on v4

--- a/solution.py
+++ b/solution.py
@@ -632,6 +632,82 @@
         pltpu.make_async_copy(part, part, ag_recv.at[k]).wait()
 
 
+def finish(
+    local, heads, experts,
+    sec, own_up, own_down, recv_up, recv_down, attn, small,
+    sec_out, qkv_out, out_out, up_out, down_out, router_out, one_out, two_out, bias_out,
+    own, got, whole, attn_v, attn_f, small_v, router_v, one_v, two_v, bias_v, sec_v, sem_own, sem_got, sem_out, sem_in, sem_small,
+):
+    pieces = [(k, e) for k in range(2) for e in range(local)]
+    sources = ((own_up, recv_up), (own_down, recv_down))
+    results = (up_out, down_out)
+
+    def incoming(i):
+        k, e = pieces[i]
+        return (
+            pltpu.make_async_copy(sources[k][0].at[e], own.at[i], sem_own.at[i]),
+            pltpu.make_async_copy(sources[k][1].at[e], got.at[i], sem_got.at[i]),
+        )
+
+    def leaving(i):
+        k, e = pieces[i]
+        return pltpu.make_async_copy(whole.at[i], results[k].at[e], sem_out.at[i])
+
+    last = [pltpu.make_async_copy(attn, attn_v, sem_in.at[0]), pltpu.make_async_copy(small, small_v, sem_in.at[1])]
+    for i in range(len(pieces)):
+        for copy in incoming(i):
+            copy.start()
+        if i == 0:
+            for copy in last:
+                copy.start()
+    pass_in = pltpu.make_async_copy(sec, sec_v, sem_in.at[2])
+    pass_out = pltpu.make_async_copy(sec_v, sec_out, sem_in.at[3])
+    pass_in.start()
+    step = 64
+    for i in range(len(pieces)):
+        for copy in incoming(i):
+            copy.wait()
+
+        def add(r, _, i=i):
+            at = pl.ds(pl.multiple_of(r * step, step), step)
+            whole[i, at] = own[i, at].astype(F32) + got[i, at].astype(F32)
+            return 0
+        lax.fori_loop(0, own.shape[1] // step, add, 0)
+        leaving(i).start()
+    pass_in.wait()
+    pass_out.start()
+    for copy in last:
+        copy.wait()
+
+    def widen(r, _):
+        attn_f[r] = attn_v[r].astype(F32)
+        return 0
+    lax.fori_loop(0, attn_f.shape[0], widen, 0)
+    cut = attn_f.shape[0] * 3 // 4
+    out = [
+        pltpu.make_async_copy(attn_f.at[pl.ds(0, cut)], qkv_out, sem_small.at[0]),
+        pltpu.make_async_copy(attn_f.at[pl.ds(cut, attn_f.shape[0] - cut)], out_out, sem_small.at[1]),
+    ]
+    for b in range(router_v.shape[1] // LANES):
+        cols = slice(b * LANES, (b + 1) * LANES)
+        at = b * SMALL
+        router_v[:, cols] = small_v[at:at + experts]
+        one_v[:, cols] = small_v[at + experts:at + experts + 1]
+        two_v[:, cols] = small_v[at + experts + 1:at + experts + 2]
+    for h in range(heads):
+        bias_v[h] = small_v[experts + 8 + h:experts + 9 + h, 0:bias_v.shape[2]]
+    out += [
+        pltpu.make_async_copy(src, dst, sem_small.at[2 + k])
+        for k, (src, dst) in enumerate(((router_v, router_out), (one_v, one_out), (two_v, two_out), (bias_v, bias_out)))
+    ]
+    for copy in out:
+        copy.start()
+    for i in range(len(pieces)):
+        leaving(i).wait()
+    for copy in (*out, pass_out):
+        copy.wait()
+
+
 def body(
     block_input, cotangent, routes, offset_bucket, norm1_gain, qkv_weight, out_weight, bias_table, norm2_gain,
     router_weight, up_weight, down_weight,
@@ -700,14 +776,28 @@
         bias_table.transpose(1, 0, 2), router_weight[0].T, qkv_weight[0].transpose(0, 2, 1), out_weight[0],
         up_weight[0], down_weight[0],
     )
-    grad_up = own_up.astype(F32) + recv_up.astype(F32)
-    grad_down = own_down.astype(F32) + recv_down.astype(F32)
-    attn = attn.reshape(4, hw, width).astype(F32)
-    small = small.reshape(width // LANES, SMALL, LANES).transpose(1, 0, 2).reshape(SMALL, width)
+    blocks = (2 * local, width, ff)
+    sec, qkv_g, out_g, up_g, down_g, router_g, one_g, two_g, bias_g = pl.pallas_call(
+        functools.partial(finish, local, heads, experts),
+        out_shape=[
+            sds((micro, seq, width), F32), sds((ne * 3 // 4, rows, width), F32), sds((ne // 4, rows, width), F32),
+            sds(half, F32), sds(half, F32), sds((experts, width), F32), sds((1, width), F32), sds((1, width), F32),
+            sds((heads, 1, buckets), F32),
+        ],
+        in_specs=[hbm] * 7,
+        out_specs=[hbm] * 9,
+        scratch_shapes=[
+            vm(blocks, BF16), vm(blocks, BF16), vm(blocks, F32), vm((ne, rows, width), BF16), vm((ne, rows, width), F32),
+            vm((flat, LANES), F32), vm((experts, width), F32), vm((1, width), F32), vm((1, width), F32),
+            vm((heads, 1, buckets), F32), vm((micro, seq, width), F32),
+            dma((2 * local,)), dma((2 * local,)), dma((2 * local,)), dma((4,)), dma((6,)),
+        ],
+        compiler_params=pltpu.CompilerParams(vmem_limit_bytes=60 * 1024 * 1024),
+        cost_estimate=pl.CostEstimate(flops=3_000_000, bytes_accessed=25_000_000, transcendentals=0),
+    )(sec, own_up, own_down, recv_up, recv_down, attn, small)
     return (
-        sec[None], small[experts][None], attn[None, :3].transpose(0, 1, 3, 2), attn[3][None],
-        small[None, experts + 8:experts + 8 + heads, :buckets], small[experts + 1][None], small[:experts].T[None],
-        grad_up[None], grad_down[None],
+        sec[None], one_g, qkv_g.reshape(1, 3, hw, width).transpose(0, 1, 3, 2), out_g.reshape(1, hw, width),
+        bias_g.transpose(1, 0, 2), two_g, router_g.T[None], up_g[None], down_g[None],
     )
 
 

time: 177 us -> 171 us (0.966)
  Pallas kernels: 161 us -> 170 us
  other arithmetic: 8.65 us -> 0 us
  local copies, waits for them, and re-layouts: 5.12 us -> 0 us
    pallas_call x0 -> x1, Pallas kernels: none -> 8.66 us  [body(): pl.pallas_call(functools.partial(finish, local, heads, experts), out_shap...]
    broadcast_in_dim x1 -> x0, other arithmetic: 8.65 us -> none  [body(): grad_down[None]]
    slice x4 -> x0, local copies, waits for them, and re-layouts: 2.83 us -> none  [the longest x1 1.38 us: body(): attn[None, :3].transpose(0, 1, 3, 2)]
    unnamed x11 -> x0, local copies, waits for them, and re-layouts: 2.16 us -> none
where the time goes in v5:
time: 171 us
  Pallas kernels  170 us (99%)
    pallas_call x1, Pallas kernels, body(): pl.pallas_call(functools.partial(kernel, (ne, nz, seq, width, local, head...  161 us
    pallas_call x1, Pallas kernels, body(): pl.pallas_call(functools.partial(finish, local, heads, experts), out_shap...  8.66 us

profile of v5, /device:TPU:0, one launch (start us, length us, event | category | flops | bytes accessed | tf_op | source)
XLA Modules:
  0.0 170.8 jit_solution(5057854908107571686)
XLA Ops:
  0.6 161.5 %shard_map.187 = (f32[2,128,768]{2,1,0:T(8,128)}, bf16[2,768,768]{2,1,0:T(8,128)(2,1)}, bf16[2,768,768]{2,1,0:T(8,128)(2,1)}, bf16[2,768,768]{2,1,0:T(8,128)(2,1...) custom-call(bf16[2,128,768]{2,1,0:T(8,128)(2,1)} %x_in.1, ...), custom_call_target="tpu_custom_call" | custom-call | flops 20000000000 | bytes 40000000 | tf_op jit(solution)/shard_map/pallas_call | solution.py:741
  162.1 8.7 %shard_map.188 = (f32[2,128,768]{2,1,0:T(8,128)}, f32[12,48,768]{2,1,0:T(8,128)}, f32[4,48,768]{2,1,0:T(8,128)}, f32[2,768,768]{2,1,0:T(8,128)}, f32[2,768,768]{...) custom-call(f32[2,128,768]{2,1,0:T(8,128)} %get-tuple-element.25.sec, ...), custom_call_target="tpu_custom_call" | custom-call | flops 3000000 | bytes 25000000 | tf_op jit(solution)/shard_map/pallas_call | solution.py:780

commit v6 on v5

--- a/solution.py
+++ b/solution.py
@@ -44,10 +44,10 @@
 def kernel(
     dims,
     x_in, cot_in, routes_in, bucket_in, one_in, two_in, bias_in, router_in, qkv_in, out_in, up_in, down_in,
-    sec_out, own_up, own_down, recv_up, recv_down, attn_out, small_out,
+    sec_out, own_up, own_down, attn_out, small_out,
     xin, cot, bucket, hot, routes, gain_one, gain_two, bias_w, router, w_qkv, w_full, w_up, w_down,
     hs, n_one, qkv, probs_s, mixed_s, h_mid_s, n_two, comb, eprobs, x_s, u_s, x_dy, x_du, hid_s, g_s, fin, dqkv,
-    send_a, recv_a, send_g, recv_g, send_c, recv_c, mix, red_a, red_c, red_g, g_up, g_down, chunk, chunk_pair, chunk_in, flat, small, small_pair,
+    send_a, recv_a, send_g, recv_g, send_c, recv_c, mix, red_a, red_c, red_g, g_up, g_down, recv_up, recv_down, chunk, chunk_pair, chunk_in, flat, small, small_pair,
     small_in, total, total_small,
     sem_in, sem_w, sem_ws, wo_send, wo_recv, mx_send, mx_recv, sa_send, sa_recv, sg_send, sg_recv, sc_send, sc_recv, rd_send, rd_recv, rc_send, rc_recv, gr_send, gr_recv, gr_loc,
     ck_send, ck_recv, pr_send, pr_recv, ag_send, ag_recv, ag_loc, sec_send, sec_recv, sec_loc,
@@ -91,6 +91,10 @@
         (one_in, gain_one), (qkv_in, w_qkv), (bias_in, bias_w), (w_full, w_full), (routes_in, routes), (router_in, router),
         (two_in, gain_two), (up_in, w_up), (down_in, w_down),
     ]
+    def to_partner(src, dst, send, recv):
+        pltpu.make_async_remote_copy(
+            src_ref=src, dst_ref=dst, send_sem=send, recv_sem=recv, device_id={"pipe": other}, device_id_type=MESH).start()
+
     def load(k):
         src, dst = weights[k]
         pltpu.make_async_copy(src.at[p] if k == 4 else src, dst.at[p], sem_w.at[k, p]).start()
@@ -106,17 +110,20 @@
 
         def one(r, _):
             pltpu.make_async_remote_copy(
-                src_ref=out_in, dst_ref=w_full.at[p, z], send_sem=wo_send, recv_sem=wo_recv,
+                src_ref=out_in, dst_ref=w_full.at[p, z], send_sem=wo_send, recv_sem=wo_recv.at[r],
                 device_id={"tensor": lax.rem(z + r, nz)}, device_id_type=MESH).start()
             return 0
         lax.fori_loop(1, nz, one, 0)
+        to_partner(out_in, w_full.at[p, z], sem_ws.at[3], sem_w.at[3, p])
 
     def gather_end():
         pltpu.make_async_copy(out_in, w_full.at[p, z], sem_in.at[3]).wait()
         part = w_full.at[p, pl.ds(1, nz - 1)]
         pltpu.make_async_copy(part, part, wo_send).wait()
-        pltpu.make_async_copy(part, part, wo_recv).wait()
-        lend(3).start()
+        for r in range(1, nz):
+            got = w_full.at[p, lax.rem(z + nz - r, nz)]
+            pltpu.make_async_copy(got, got, wo_recv.at[r]).wait()
+            to_partner(got, got, sem_ws.at[3], sem_w.at[3, p])
 
     load(4)
 
@@ -140,7 +147,8 @@
         pltpu.make_async_copy(dst.at[l], dst.at[l], sem_w.at[k, l]).wait()
 
     def send_all(src, dst, send, recv, forth):
-        def one(r, _):
+        def one(i, _):
+            r = ne - i
             pltpu.make_async_remote_copy(
                 src_ref=src.at[r], dst_ref=dst.at[r], send_sem=send, recv_sem=recv,
                 device_id={"expert": lax.rem(x + r if forth else x + ne - r, ne)}, device_id_type=MESH).start()
@@ -169,12 +177,10 @@
         return recv_c[l, kind, c].reshape(slots, part_w)
 
     def reduce_start(buf, send, recv):
-        def one(r, _):
+        for r in sorted(range(1, nz), key=lambda r: -min(r, nz - r)):
             pltpu.make_async_remote_copy(
                 src_ref=buf.at[0], dst_ref=buf.at[r], send_sem=send, recv_sem=recv,
                 device_id={"tensor": lax.rem(z + r, nz)}, device_id_type=MESH).start()
-            return 0
-        lax.fori_loop(1, nz, one, 0)
 
     def reduce_end(buf, send, recv):
         part = buf.at[pl.ds(1, nz - 1)]
@@ -380,12 +386,25 @@
     def piece(ref, j):
         return ref.at[pl.ds(pl.multiple_of(j * flat_rows, 8), flat_rows)]
 
+    def sum_experts():
+        step = 64
+        for k, (mine, theirs, dst) in enumerate(((g_up, recv_up, own_up), (g_down, recv_down, own_down))):
+            pltpu.make_async_copy(theirs, theirs, gr_recv.at[k]).wait()
+            for e in range(local):
+                def add(r, _, mine=mine, theirs=theirs, e=e):
+                    at = pl.ds(pl.multiple_of(r * step, step), step)
+                    mine[p, e, at] = (mine[p, e, at].astype(F32) + theirs[e, at].astype(F32)).astype(BF16)
+                    return 0
+                lax.fori_loop(0, theirs.shape[1] // step, add, 0)
+            pltpu.make_async_copy(mine.at[p], dst, gr_loc.at[k]).start()
+
     def merge_attn():
         pltpu.make_async_copy(chunk_pair, chunk_pair, pr_recv.at[0]).wait()
         for c in range(parts_c):
             chunk_pair[c] = (chunk[p, c].astype(F32) + chunk_pair[c].astype(F32)).astype(BF16)
 
-            def scatter(r, _, c=c):
+            def scatter(i, _, c=c):
+                r = ne - i
                 to = lax.rem(x + r, ne)
                 pltpu.make_async_remote_copy(
                     src_ref=chunk_pair.at[c, to], dst_ref=chunk_in.at[c, r], send_sem=ck_send.at[c], recv_sem=ck_recv.at[c],
@@ -398,7 +417,8 @@
         pltpu.make_async_copy(small_pair, small_pair, pr_recv.at[1]).wait()
         small_pair[...] = small[p] + small_pair[...]
 
-        def scatter(r, _):
+        def scatter(i, _):
+            r = ne - i
             to = lax.rem(x + r, ne)
             pltpu.make_async_remote_copy(
                 src_ref=piece(small_pair, to), dst_ref=small_in.at[r], send_sem=ck_send.at[parts_c], recv_sem=ck_recv.at[parts_c],
@@ -420,7 +440,7 @@
         def one(r, _):
             pltpu.make_async_remote_copy(
                 src_ref=whole, dst_ref=dst, send_sem=ag_send.at[k], recv_sem=ag_recv.at[k],
-                device_id={"expert": lax.rem(x + r, ne)}, device_id_type=MESH).start()
+                device_id={"expert": lax.rem(x + ne - r, ne)}, device_id_type=MESH).start()
             return 0
         lax.fori_loop(1, ne, one, 0)
 
@@ -430,10 +450,6 @@
 
     def spread_small():
         spread(parts_c, small_in, total_small, piece(small_out, x))
-
-    def to_partner(src, dst, send, recv):
-        pltpu.make_async_remote_copy(
-            src_ref=src, dst_ref=dst, send_sem=send, recv_sem=recv, device_id={"pipe": other}, device_id_type=MESH).start()
 
     part = send_a.at[1, pl.ds(1, ne - 1)]
     pltpu.make_async_copy(part, part, sa_send.at[1, 1]).wait()
@@ -444,6 +460,11 @@
         value = value.astype(BF16)
         for c in range(parts_c):
             chunk[l, c, k * per:(k + 1) * per] = value[:, c * part_w:(c + 1) * part_w].reshape(per, rows, part_w)
+
+        @pl.when(p != l)
+        def _():
+            at = pl.ds(k * per, per)
+            to_partner(chunk.at[l, :, at], chunk_pair.at[:, at], pr_send.at[0], pr_recv.at[0])
 
     def backward(i, _):
         l = 1 - i
@@ -494,6 +515,7 @@
         def _():
             spread_attn()
             spread_small()
+            sum_experts()
 
         gg = jnp.zeros((seq, LANES), F32)
         for kk in range(2):
@@ -515,11 +537,6 @@
 
         both = comb[l, 0:seq] + comb[l, seq:2 * seq]
         dn2 = summed_back(1, l, lambda back: nn(both, back))
-
-        @pl.when(p == l)
-        def _():
-            pltpu.make_async_copy(g_up.at[l], own_up, gr_loc.at[0]).start()
-            pltpu.make_async_copy(g_down.at[l], own_down, gr_loc.at[1]).start()
 
         @pl.when(p != l)
         def _():
@@ -577,13 +594,10 @@
         for c in range(3):
             keep_grad(l, c, tn(dqkv[c], n1))
 
-        @pl.when(p != l)
-        def _():
-            to_partner(chunk.at[l], chunk_pair, pr_send.at[0], pr_recv.at[0])
-
         @pl.when((p == 0) & (l == 0))
         def _():
             merge_attn()
+            sum_experts()
 
         bias_high = bias_g.astype(BF16)
         bias_low = (bias_g - bias_high.astype(F32)).astype(BF16)
@@ -618,7 +632,7 @@
     for k in range(len(weights)):
         lend(k).wait_send()
     for k, ref in enumerate((g_up, g_down)):
-        for sem in (gr_loc, gr_send, gr_recv):
+        for sem in (gr_loc, gr_send):
             pltpu.make_async_copy(ref.at[0], ref.at[0], sem.at[k]).wait()
     for sem in (sec_loc, sec_send, sec_recv):
         pltpu.make_async_copy(fin, fin, sem).wait()
@@ -634,20 +648,17 @@
 
 def finish(
     local, heads, experts,
-    sec, own_up, own_down, recv_up, recv_down, attn, small,
+    sec, own_up, own_down, attn, small,
     sec_out, qkv_out, out_out, up_out, down_out, router_out, one_out, two_out, bias_out,
-    own, got, whole, attn_v, attn_f, small_v, router_v, one_v, two_v, bias_v, sec_v, sem_own, sem_got, sem_out, sem_in, sem_small,
+    own, whole, attn_v, attn_f, small_v, router_v, one_v, two_v, bias_v, sec_v, sem_own, sem_out, sem_in, sem_small,
 ):
     pieces = [(k, e) for k in range(2) for e in range(local)]
-    sources = ((own_up, recv_up), (own_down, recv_down))
+    sources = (own_up, own_down)
     results = (up_out, down_out)
 
     def incoming(i):
         k, e = pieces[i]
-        return (
-            pltpu.make_async_copy(sources[k][0].at[e], own.at[i], sem_own.at[i]),
-            pltpu.make_async_copy(sources[k][1].at[e], got.at[i], sem_got.at[i]),
-        )
+        return pltpu.make_async_copy(sources[k].at[e], own.at[i], sem_own.at[i])
 
     def leaving(i):
         k, e = pieces[i]
@@ -655,8 +666,7 @@
 
     last = [pltpu.make_async_copy(attn, attn_v, sem_in.at[0]), pltpu.make_async_copy(small, small_v, sem_in.at[1])]
     for i in range(len(pieces)):
-        for copy in incoming(i):
-            copy.start()
+        incoming(i).start()
         if i == 0:
             for copy in last:
                 copy.start()
@@ -665,14 +675,13 @@
     pass_in.start()
     step = 64
     for i in range(len(pieces)):
-        for copy in incoming(i):
-            copy.wait()
-
-        def add(r, _, i=i):
+        incoming(i).wait()
+
+        def convert(r, _, i=i):
             at = pl.ds(pl.multiple_of(r * step, step), step)
-            whole[i, at] = own[i, at].astype(F32) + got[i, at].astype(F32)
+            whole[i, at] = own[i, at].astype(F32)
             return 0
-        lax.fori_loop(0, own.shape[1] // step, add, 0)
+        lax.fori_loop(0, own.shape[1] // step, convert, 0)
         leaving(i).start()
     pass_in.wait()
     pass_out.start()
@@ -738,14 +747,14 @@
     parts_in = (2, 2, PARTS, ne, 2 * CAP, part_w)
     half = (local, width, ff)
     cut = (PARTS, ne, rows, part_w)
-    sec, own_up, own_down, recv_up, recv_down, attn, small = pl.pallas_call(
+    sec, own_up, own_down, attn, small = pl.pallas_call(
         functools.partial(kernel, (ne, nz, seq, width, local, heads, ff, hd)),
         out_shape=[
-            sds((micro, seq, width), F32), sds(half, BF16), sds(half, BF16), sds(half, BF16), sds(half, BF16),
+            sds((micro, seq, width), F32), sds(half, BF16), sds(half, BF16),
             sds((ne, rows, width), BF16), sds((flat, LANES), F32),
         ],
         in_specs=[hbm] * 12,
-        out_specs=[any_space] * 7,
+        out_specs=[any_space] * 5,
         scratch_shapes=[
             vm((seq, width), BF16), vm((seq, width), BF16), vm((1, seq), jnp.int32), vm((seq, buckets), F32),
             vm((2, 2, seq), jnp.int32), vm((2, 1, width), F32), vm((2, 1, width), F32), vm((2, heads, 1, buckets), F32),
@@ -760,10 +769,10 @@
             vm((2, ne, 2 * CAP, width), BF16), vm((2, 2, ne, 2 * CAP, width), BF16), vm((ne, 2 * CAP, LANES), BF16),
             vm((ne, 2 * CAP, LANES), BF16), vm(parts_in[2:], BF16), vm(parts_in, BF16),
             vm((2, nz, seq, hw), BF16), vm((2, nz, seq, width), BF16), vm((2, 2, PARTS, nz, seq, part_w), BF16), vm((2, nz, seq, LANES), BF16),
-            vm((2, *half), BF16), vm((2, *half), BF16), vm((2, *cut), BF16), vm(cut, BF16),
+            vm((2, *half), BF16), vm((2, *half), BF16), vm(half, BF16), vm(half, BF16), vm((2, *cut), BF16), vm(cut, BF16),
             vm(cut, BF16), vm((SMALL, width), F32), vm((2, flat, LANES), F32), vm((flat, LANES), F32),
             vm((ne, flat // ne, LANES), F32), vm((PARTS, rows, part_w), BF16), vm((flat // ne, LANES), F32),
-            dma((4,)), dma((9, 2)), dma((9,)), dma, dma, dma((2,)), dma((2,)), dma((2, 2)), dma((2, 2)), dma, dma, dma((2, 2, PARTS)), dma((2, 2, PARTS)),
+            dma((4,)), dma((9, 2)), dma((9,)), dma, dma((4,)), dma((2,)), dma((2,)), dma((2, 2)), dma((2, 2)), dma, dma, dma((2, 2, PARTS)), dma((2, 2, PARTS)),
             dma((2, 2)), dma((2, 2)), dma((2, 2, PARTS)), dma((2, 2, PARTS)), dma((2,)), dma((2,)), dma((2,)),
             dma((PARTS + 1,)), dma((PARTS + 1,)), dma((2,)), dma((2,)), dma((PARTS + 1,)), dma((PARTS + 1,)), dma((PARTS + 1,)),
             dma, dma, dma,
@@ -784,17 +793,17 @@
             sds(half, F32), sds(half, F32), sds((experts, width), F32), sds((1, width), F32), sds((1, width), F32),
             sds((heads, 1, buckets), F32),
         ],
-        in_specs=[hbm] * 7,
+        in_specs=[hbm] * 5,
         out_specs=[hbm] * 9,
         scratch_shapes=[
-            vm(blocks, BF16), vm(blocks, BF16), vm(blocks, F32), vm((ne, rows, width), BF16), vm((ne, rows, width), F32),
+            vm(blocks, BF16), vm(blocks, F32), vm((ne, rows, width), BF16), vm((ne, rows, width), F32),
             vm((flat, LANES), F32), vm((experts, width), F32), vm((1, width), F32), vm((1, width), F32),
             vm((heads, 1, buckets), F32), vm((micro, seq, width), F32),
-            dma((2 * local,)), dma((2 * local,)), dma((2 * local,)), dma((4,)), dma((6,)),
+            dma((2 * local,)), dma((2 * local,)), dma((4,)), dma((6,)),
         ],
         compiler_params=pltpu.CompilerParams(vmem_limit_bytes=60 * 1024 * 1024),
         cost_estimate=pl.CostEstimate(flops=3_000_000, bytes_accessed=25_000_000, transcendentals=0),
-    )(sec, own_up, own_down, recv_up, recv_down, attn, small)
+    )(sec, own_up, own_down, attn, small)
     return (
         sec[None], one_g, qkv_g.reshape(1, 3, hw, width).transpose(0, 1, 3, 2), out_g.reshape(1, hw, width),
         bias_g.transpose(1, 0, 2), two_g, router_g.T[None], up_g[None], down_g[None],

time: 171 us -> 161 us (0.942)
  Pallas kernels: 170 us -> 160 us
    pallas_call x1, Pallas kernels: 161 us -> 154 us  [body(): pl.pallas_call(functools.partial(kernel, (ne, nz, seq, width, local, head...]
    pallas_call x1, Pallas kernels: 8.66 us -> 6.28 us  [body(): pl.pallas_call(functools.partial(finish, local, heads, experts), out_shap...]
where the time goes in v6:
time: 161 us
  Pallas kernels  160 us (99%)
    pallas_call x1, Pallas kernels, body(): pl.pallas_call(functools.partial(kernel, (ne, nz, seq, width, local, head...  154 us
    pallas_call x1, Pallas kernels, body(): pl.pallas_call(functools.partial(finish, local, heads, experts), out_shap...  6.28 us

profile of v6, /device:TPU:0, one launch (start us, length us, event | category | flops | bytes accessed | tf_op | source)
XLA Modules:
  0.0 161.0 jit_solution(12129174678381446736)
XLA Ops:
  0.6 154.1 %shard_map.187 = (f32[2,128,768]{2,1,0:T(8,128)}, bf16[2,768,768]{2,1,0:T(8,128)(2,1)}, bf16[2,768,768]{2,1,0:T(8,128)(2,1)}, bf16[16,48,768]{2,1,0:T(8,128)(2,1)}, f32[384,128]{1,0:T(8,128)}) custom-call(bf16[2,128,768]{2,1,0:T(8,128)(2,1)} %x_in.1, bf16[2,128,768]{2,1,0:T(8,128)(2,1)} %cot_in.1, s32[2,2,128]{2,1,0:T(2,128)} %bitcast.36, ...), custom_call_target="tpu_custom_call" | custom-call | flops 20000000000 | bytes 40000000 | tf_op jit(solution)/shard_map/pallas_call | solution.py:750
  154.7 6.3 %shard_map.188 = (f32[2,128,768]{2,1,0:T(8,128)}, f32[12,48,768]{2,1,0:T(8,128)}, f32[4,48,768]{2,1,0:T(8,128)}, f32[2,768,768]{2,1,0:T(8,128)}, f32[2,768,768]{...) custom-call(f32[2,128,768]{2,1,0:T(8,128)} %get-tuple-element.23.sec, ...), custom_call_target="tpu_custom_call" | custom-call | flops 3000000 | bytes 25000000 | tf_op jit(solution)/shard_map/pallas_call | solution.py:789

commit v7 on v6

--- a/solution.py
+++ b/solution.py
@@ -14,7 +14,8 @@
 BF16 = jnp.bfloat16
 LANES = 128
 CAP = 8
-PARTS = 3
+PARTS = 6
+CUTS = 6
 SMALL = 64
 VMEM_MB = 60
 TANH_A = 0.7978845608
@@ -62,6 +63,7 @@
     rows = width // ne
     parts_c = PARTS
     part_w = width // parts_c
+    cut_w = width // CUTS
     fold = width // LANES
     per = hw // rows
     flat_rows = fold * SMALL // ne
@@ -400,7 +402,7 @@
 
     def merge_attn():
         pltpu.make_async_copy(chunk_pair, chunk_pair, pr_recv.at[0]).wait()
-        for c in range(parts_c):
+        for c in range(CUTS):
             chunk_pair[c] = (chunk[p, c].astype(F32) + chunk_pair[c].astype(F32)).astype(BF16)
 
             def scatter(i, _, c=c):
@@ -421,7 +423,7 @@
             r = ne - i
             to = lax.rem(x + r, ne)
             pltpu.make_async_remote_copy(
-                src_ref=piece(small_pair, to), dst_ref=small_in.at[r], send_sem=ck_send.at[parts_c], recv_sem=ck_recv.at[parts_c],
+                src_ref=piece(small_pair, to), dst_ref=small_in.at[r], send_sem=ck_send.at[CUTS], recv_sem=ck_recv.at[CUTS],
                 device_id={"expert": to}, device_id_type=MESH).start()
             return 0
         lax.fori_loop(1, ne, scatter, 0)
@@ -445,11 +447,11 @@
         lax.fori_loop(1, ne, one, 0)
 
     def spread_attn():
-        for c in range(parts_c):
-            spread(c, chunk_in.at[c], total.at[c], attn_out.at[x, :, pl.ds(c * part_w, part_w)])
+        for c in range(CUTS):
+            spread(c, chunk_in.at[c], total.at[c], attn_out.at[x, :, pl.ds(c * cut_w, cut_w)])
 
     def spread_small():
-        spread(parts_c, small_in, total_small, piece(small_out, x))
+        spread(CUTS, small_in, total_small, piece(small_out, x))
 
     part = send_a.at[1, pl.ds(1, ne - 1)]
     pltpu.make_async_copy(part, part, sa_send.at[1, 1]).wait()
@@ -458,8 +460,8 @@
 
     def keep_grad(l, k, value):
         value = value.astype(BF16)
-        for c in range(parts_c):
-            chunk[l, c, k * per:(k + 1) * per] = value[:, c * part_w:(c + 1) * part_w].reshape(per, rows, part_w)
+        for c in range(CUTS):
+            chunk[l, c, k * per:(k + 1) * per] = value[:, c * cut_w:(c + 1) * cut_w].reshape(per, rows, cut_w)
 
         @pl.when(p != l)
         def _():
@@ -638,8 +640,8 @@
         pltpu.make_async_copy(fin, fin, sem).wait()
     for k, pair in enumerate((chunk_pair, small_pair)):
         pltpu.make_async_copy(pair, pair, pr_send.at[k]).wait()
-    for k in range(parts_c + 1):
-        whole, arrived_at = (total.at[k], chunk_in.at[k]) if k < parts_c else (total_small, small_in)
+    for k in range(CUTS + 1):
+        whole, arrived_at = (total.at[k], chunk_in.at[k]) if k < CUTS else (total_small, small_in)
         pltpu.make_async_copy(whole, whole, ag_loc.at[k]).wait()
         part = arrived_at.at[pl.ds(1, ne - 1)]
         pltpu.make_async_copy(part, part, ag_send.at[k]).wait()
@@ -732,6 +734,7 @@
     rows = width // ne
     parts_c = PARTS
     part_w = width // parts_c
+    cut_w = width // CUTS
     fold = width // LANES
     per = hw // rows
     flat_rows = fold * SMALL // ne
@@ -746,7 +749,7 @@
     flat = width // LANES * SMALL
     parts_in = (2, 2, PARTS, ne, 2 * CAP, part_w)
     half = (local, width, ff)
-    cut = (PARTS, ne, rows, part_w)
+    cut = (CUTS, ne, rows, width // CUTS)
     sec, own_up, own_down, attn, small = pl.pallas_call(
         functools.partial(kernel, (ne, nz, seq, width, local, heads, ff, hd)),
         out_shape=[
@@ -771,10 +774,10 @@
             vm((2, nz, seq, hw), BF16), vm((2, nz, seq, width), BF16), vm((2, 2, PARTS, nz, seq, part_w), BF16), vm((2, nz, seq, LANES), BF16),
             vm((2, *half), BF16), vm((2, *half), BF16), vm(half, BF16), vm(half, BF16), vm((2, *cut), BF16), vm(cut, BF16),
             vm(cut, BF16), vm((SMALL, width), F32), vm((2, flat, LANES), F32), vm((flat, LANES), F32),
-            vm((ne, flat // ne, LANES), F32), vm((PARTS, rows, part_w), BF16), vm((flat // ne, LANES), F32),
+            vm((ne, flat // ne, LANES), F32), vm((CUTS, rows, width // CUTS), BF16), vm((flat // ne, LANES), F32),
             dma((4,)), dma((9, 2)), dma((9,)), dma, dma((4,)), dma((2,)), dma((2,)), dma((2, 2)), dma((2, 2)), dma, dma, dma((2, 2, PARTS)), dma((2, 2, PARTS)),
             dma((2, 2)), dma((2, 2)), dma((2, 2, PARTS)), dma((2, 2, PARTS)), dma((2,)), dma((2,)), dma((2,)),
-            dma((PARTS + 1,)), dma((PARTS + 1,)), dma((2,)), dma((2,)), dma((PARTS + 1,)), dma((PARTS + 1,)), dma((PARTS + 1,)),
+            dma((CUTS + 1,)), dma((CUTS + 1,)), dma((2,)), dma((2,)), dma((CUTS + 1,)), dma((CUTS + 1,)), dma((CUTS + 1,)),
             dma, dma, dma,
         ],
         compiler_params=pltpu.CompilerParams(

time: 161 us -> 160 us (level)
  no operation moved by 1% of the time
where the time goes in v7:
time: 160 us; the launch traced here: 159 us
  Pallas kernels  159 us (99%)
    pallas_call x1, Pallas kernels, body(): pl.pallas_call(functools.partial(kernel, (ne, nz, seq, width, local, head...  153 us
    pallas_call x1, Pallas kernels, body(): pl.pallas_call(functools.partial(finish, local, heads, experts), out_shap...  6.28 us

profile of v7, /device:TPU:0, one launch (start us, length us, event | category | flops | bytes accessed | tf_op | source)
XLA Modules:
  0.0 159.5 jit_solution(10882352173652991540)
XLA Ops:
  0.6 152.6 %shard_map.187 = (f32[2,128,768]{2,1,0:T(8,128)}, bf16[2,768,768]{2,1,0:T(8,128)(2,1)}, bf16[2,768,768]{2,1,0:T(8,128)(2,1)}, bf16[16,48,768]{2,1,0:T(8,128)(2,1)}, f32[384,128]{1,0:T(8,128)}) custom-call(bf16[2,128,768]{2,1,0:T(8,128)(2,1)} %x_in.1, bf16[2,128,768]{2,1,0:T(8,128)(2,1)} %cot_in.1, s32[2,2,128]{2,1,0:T(2,128)} %bitcast.36, ...), custom_call_target="tpu_custom_call" | custom-call | flops 20000000000 | bytes 40000000 | tf_op jit(solution)/shard_map/pallas_call | solution.py:753
  153.2 6.3 %shard_map.188 = (f32[2,128,768]{2,1,0:T(8,128)}, f32[12,48,768]{2,1,0:T(8,128)}, f32[4,48,768]{2,1,0:T(8,128)}, f32[2,768,768]{2,1,0:T(8,128)}, f32[2,768,768]{...) custom-call(f32[2,128,768]{2,1,0:T(8,128)} %get-tuple-element.23.sec, ...), custom_call_target="tpu_custom_call" | custom-call | flops 3000000 | bytes 25000000 | tf_op jit(solution)/shard_map/pallas_call | solution.py:792

commit v8 on v7

--- a/solution.py
+++ b/solution.py
@@ -138,8 +138,10 @@
 
     @pl.when(p == 0)
     def _():
+        for k in (0, 1):
+            lend(k).start()
         gather_start()
-        for k in (0, 1, 2, 5, 6, 7, 8):
+        for k in (2, 5, 6, 7, 8):
             lend(k).start()
         for k in (7, 8):
             load(k)
@@ -568,8 +570,6 @@
         dv = jnp.zeros((seq, hw), F32)
         causal = lanes_of((seq, seq), 0) >= lanes_of((seq, seq), 1)
         row_at = lanes_of((seq, seq), 0)
-        top = lanes_of((8, LANES), 0)
-        bias_g = jnp.zeros((8, LANES), F32)
         for h in range(heads):
             mask = head_mask(h)
             prob = probs_s[l, h]
@@ -579,12 +579,7 @@
             ds = jnp.where(causal, prob * (dp - jnp.sum(prob * dp, -1, keepdims=True)), 0.0).astype(BF16)
             dq = dq + nn(ds, k * mask)
             dk = dk + tn(ds, q * mask)
-            turned = ds.astype(F32)
-            bit = 1
-            while bit < seq:
-                turned = jnp.where((row_at & bit) != 0, pltpu.roll(turned, seq - bit, 1), turned)
-                bit *= 2
-            bias_g = bias_g + jnp.where(top == h, jnp.sum(turned, 0, keepdims=True), 0.0)
+            probs_s[l, h] = ds.astype(F32)
         dqkv[0] = (dq * (hd ** -0.5)).astype(BF16)
         dqkv[1] = (dk * (hd ** -0.5)).astype(BF16)
         dqkv[2] = dv.astype(BF16)
@@ -601,6 +596,15 @@
             merge_attn()
             sum_experts()
 
+        top = lanes_of((8, LANES), 0)
+        bias_g = jnp.zeros((8, LANES), F32)
+        for h in range(heads):
+            turned = probs_s[l, h]
+            bit = 1
+            while bit < seq:
+                turned = jnp.where((row_at & bit) != 0, pltpu.roll(turned, seq - bit, 1), turned)
+                bit *= 2
+            bias_g = bias_g + jnp.where(top == h, jnp.sum(turned, 0, keepdims=True), 0.0)
         bias_high = bias_g.astype(BF16)
         bias_low = (bias_g - bias_high.astype(F32)).astype(BF16)
         hot_b = hot[...].astype(BF16)

time: 160 us -> 159 us (level)
  no operation moved by 1% of the time
where the time goes in v8:
time: 159 us; the launch traced here: 158 us
  Pallas kernels  158 us (99%)
    pallas_call x1, Pallas kernels, body(): pl.pallas_call(functools.partial(kernel, (ne, nz, seq, width, local, head...  151 us
    pallas_call x1, Pallas kernels, body(): pl.pallas_call(functools.partial(finish, local, heads, experts), out_shap...  6.28 us

profile of v8, /device:TPU:0, one launch (start us, length us, event | category | flops | bytes accessed | tf_op | source)
XLA Modules:
  0.0 158.2 jit_solution(12088729163807779325)
XLA Ops:
  0.6 151.3 %shard_map.187 = (f32[2,128,768]{2,1,0:T(8,128)}, bf16[2,768,768]{2,1,0:T(8,128)(2,1)}, bf16[2,768,768]{2,1,0:T(8,128)(2,1)}, bf16[16,48,768]{2,1,0:T(8,128)(2,1)}, f32[384,128]{1,0:T(8,128)}) custom-call(bf16[2,128,768]{2,1,0:T(8,128)(2,1)} %x_in.1, bf16[2,128,768]{2,1,0:T(8,128)(2,1)} %cot_in.1, s32[2,2,128]{2,1,0:T(2,128)} %bitcast.36, ...), custom_call_target="tpu_custom_call" | custom-call | flops 20000000000 | bytes 40000000 | tf_op jit(solution)/shard_map/pallas_call | solution.py:757
  151.9 6.3 %shard_map.188 = (f32[2,128,768]{2,1,0:T(8,128)}, f32[12,48,768]{2,1,0:T(8,128)}, f32[4,48,768]{2,1,0:T(8,128)}, f32[2,768,768]{2,1,0:T(8,128)}, f32[2,768,768]{...) custom-call(f32[2,128,768]{2,1,0:T(8,128)} %get-tuple-element.23.sec, ...), custom_call_target="tpu_custom_call" | custom-call | flops 3000000 | bytes 25000000 | tf_op jit(solution)/shard_map/pallas_call | solution.py:796
